TPU v7x, 32 devices: a whole 2x2x4 slice. The times are simulated.
32 devices in a mesh: seq: 8 (over z, y), head: 4 (over x, core).
Axes of the slice: x: 2, y: 2, z: 4, core: 2. Of those that a mesh axis runs over, the one named last changes fastest.
Arguments:
- q_in: bfloat16 [1024, 2048], P(('seq', 'head')), may hold values from -52 to 52
- k_in: bfloat16 [1024, 2048], P(('seq', 'head')), may hold values from -6 to 6
- v_in: bfloat16 [1024, 2048], P(('seq', 'head')), may hold values from -6 to 6
- grad_out: bfloat16 [1024, 2048], P(('seq', 'head')), may hold values from -6 to 6
- positions: int32 [3, 1024], P(None, 'seq'), may hold values from 0 to 79, as said below
- views: int32 [1024], replicated, may hold values from 0 to 5, as said below
- adjacency: int32 [6, 2], replicated, may hold values from 0 to 5, as said below
Outputs:
- attended: bfloat16 [1024, 2048], P('seq', 'head')
- grad_q: bfloat16 [1024, 2048], P('seq', 'head')
- grad_k: bfloat16 [1024, 2048], P('seq', 'head')
- grad_v: bfloat16 [1024, 2048], P('seq', 'head')
Inputs may be any that keep to these rules, and one draw needn't show every extreme that they name: `positions`: time ids lie below 16, height ids below 44, width ids below 80. `views`: never decreasing, starting at 0; a view changes only at a multiple of 128 rows; each view holds the rows of 1 device or of one device more, and which views hold one more is drawn. `adjacency`: the two entries of a view are distinct other views; the relation is symmetric and joins all views in one closed cycle.
All inputs are finite; a program needn't handle non-finite values.
Results may differ from a plain program's by a relative error of at most 0.025.
Values may be sent and summed in bfloat16 or wider, within the bound.
No kernel may reach another device: no remote copies, remote signals or barrier semaphores. Data moves between devices by JAX's collectives and lax.ppermute only.
A program may use at most 64 MiB of HBM per device.

v0:
```python
import jax
import jax.numpy as jnp
from jax import lax
from jax.sharding import PartitionSpec as P

HD = 128


NEG = -1e30
THETA = 10000.0


def rope_tables(positions, width):
    side = width // 6 * 2
    first = width - 2 * side
    parts = []
    for row, group in ((0, first), (1, side), (2, side)):
        steps = jnp.arange(group // 2, dtype=jnp.float32)
        inverse = THETA ** (-2.0 * steps / group)
        parts.append(positions[row].astype(jnp.float32)[:, None] * inverse[None, :])
    angles = jnp.concatenate(parts, axis=1)
    return (jnp.cos(angles), jnp.sin(angles))


def rotate(values, cosine, sine, sign):
    half = values.shape[-1] // 2
    first = values[..., :half]
    second = values[..., half:]
    return jnp.concatenate(
        [first * cosine - sign * second * sine, sign * first * sine + second * cosine], axis=-1
    )


def neighbours(view_ids, adjacency):
    count = adjacency.shape[0]
    match = view_ids[:, None] == jnp.arange(count, dtype=jnp.int32)[None, :]
    near_one = jnp.sum(jnp.where(match, adjacency[None, :, 0], 0), axis=1)
    near_two = jnp.sum(jnp.where(match, adjacency[None, :, 1], 0), axis=1)
    return (near_one, near_two)


def in_blocks(pieces, carry, step):
    count = pieces[0].shape[0]
    size = count
    while size > 1024 and size % 2 == 0:
        size = size // 2
    number = count // size
    shaped = tuple((piece.reshape((number, size) + piece.shape[1:]) for piece in pieces))
    firsts = size * jnp.arange(number, dtype=jnp.int32)

    def advance(state, item):
        return (step(state, item[0], item[1]), None)

    final, _ = lax.scan(advance, carry, (shaped, firsts))
    return final


def on_device(q_in, k_in, v_in, grad_out, positions, views, adjacency):
    query, keys, values, grads = (
        lax.all_to_all(q_in, "head", split_axis=1, concat_axis=0, tiled=True),
        lax.all_to_all(k_in, "head", split_axis=1, concat_axis=0, tiled=True),
        lax.all_to_all(v_in, "head", split_axis=1, concat_axis=0, tiled=True),
        lax.all_to_all(grad_out, "head", split_axis=1, concat_axis=0, tiled=True),
    )
    rows, width = query.shape
    heads = width // HD
    scale = HD ** (-0.5)
    cosine, sine = rope_tables(positions, HD)
    cosine = cosine[:, None, :]
    sine = sine[:, None, :]
    query_rot = rotate(
        query.reshape(rows, heads, HD).astype(jnp.float32), cosine, sine, 1.0
    ).astype(jnp.bfloat16)
    key_rot = rotate(keys.reshape(rows, heads, HD).astype(jnp.float32), cosine, sine, 1.0).astype(
        jnp.bfloat16
    )
    value_split = values.reshape(rows, heads, HD)
    grad_split = grads.reshape(rows, heads, HD)
    first_row = lax.axis_index("seq") * rows
    own_views = lax.dynamic_slice_in_dim(views, first_row, rows)
    near_one, near_two = neighbours(own_views, adjacency)
    every_one, every_two = neighbours(views, adjacency)

    def allowed_keys(start, count):
        other = lax.dynamic_slice_in_dim(views, start, count)[None, :]
        return (
            (other == own_views[:, None])
            | (other == near_one[:, None])
            | (other == near_two[:, None])
        )

    def scores_for(key_block, allow):
        scores = (
            jnp.einsum("qhd,khd->hqk", query_rot, key_block, preferred_element_type=jnp.float32)
            * scale
        )
        return jnp.where(allow[None], scores, NEG)

    def soft_update(top, total, accum, block, start):
        key_block, value_block = block
        allow = allowed_keys(start, key_block.shape[0])
        scores = scores_for(key_block, allow)
        new_top = jnp.maximum(top, jnp.max(scores, axis=2))
        shrink = jnp.exp(top - new_top)
        weights = jnp.where(allow[None], jnp.exp(scores - new_top[..., None]), 0.0)
        total = total * shrink + jnp.sum(weights, axis=2)
        accum = accum * shrink[..., None] + jnp.einsum(
            "hqk,khd->hqd",
            weights.astype(jnp.bfloat16),
            value_block,
            preferred_element_type=jnp.float32,
        )
        return (new_top, total, accum, weights, shrink)

    top_init = jnp.full((heads, rows), NEG, jnp.float32)
    total_init = jnp.zeros((heads, rows), jnp.float32)
    accum_init = jnp.zeros((heads, rows, HD), jnp.float32)

    def step(inner, block, bstart):
        top, total, accum, weights, shrink = soft_update(
            inner[0], inner[1], inner[2], block, bstart
        )
        return (top, total, accum)

    top, total, accum = in_blocks(
        (
            lax.all_gather(key_rot, "seq", axis=0, tiled=True),
            lax.all_gather(value_split, "seq", axis=0, tiled=True),
        ),
        (top_init, total_init, accum_init),
        step,
    )
    output = accum / total[..., None]
    finish_level = top + jnp.log(total)
    finish_delta = jnp.sum(
        grad_split.astype(jnp.float32) * jnp.transpose(output, (1, 0, 2)), axis=2
    ).T
    output, level, delta = (output, finish_level, finish_delta)

    def step(inner, block, bstart):
        key_block, value_block = block
        allow = allowed_keys(bstart, key_block.shape[0])
        scores = scores_for(key_block, allow)
        probs = jnp.where(allow[None], jnp.exp(scores - level[..., None]), 0.0)
        dprobs = jnp.einsum(
            "qhd,khd->hqk", grad_split, value_block, preferred_element_type=jnp.float32
        )
        dscores = (probs * (dprobs - delta[..., None])).astype(jnp.bfloat16)
        return inner + jnp.einsum(
            "hqk,khd->hqd", dscores, key_block, preferred_element_type=jnp.float32
        )

    grad_query = (
        in_blocks(
            (
                lax.all_gather(key_rot, "seq", axis=0, tiled=True),
                lax.all_gather(value_split, "seq", axis=0, tiled=True),
            ),
            accum_init,
            step,
        )
        * scale
    )
    level_all, delta_all = (
        lax.all_gather(level.T, "seq", axis=0, tiled=True),
        lax.all_gather(delta.T, "seq", axis=0, tiled=True),
    )

    def step(inner, block, bstart):
        grad_key, grad_value = inner
        query_block, grad_block = block
        count = query_block.shape[0]
        query_views = lax.dynamic_slice_in_dim(views, bstart, count)[None, :]
        query_one = lax.dynamic_slice_in_dim(every_one, bstart, count)[None, :]
        query_two = lax.dynamic_slice_in_dim(every_two, bstart, count)[None, :]
        mine = own_views[:, None]
        allow = (mine == query_views) | (mine == query_one) | (mine == query_two)
        level_block = lax.dynamic_slice_in_dim(level_all, bstart, count).T
        delta_block = lax.dynamic_slice_in_dim(delta_all, bstart, count).T
        scores = (
            jnp.einsum("khd,qhd->hkq", key_rot, query_block, preferred_element_type=jnp.float32)
            * scale
        )
        probs = jnp.where(allow[None], jnp.exp(scores - level_block[:, None, :]), 0.0)
        grad_value = grad_value + jnp.einsum(
            "hkq,qhd->hkd",
            probs.astype(jnp.bfloat16),
            grad_block,
            preferred_element_type=jnp.float32,
        )
        dprobs = jnp.einsum(
            "khd,qhd->hkq", value_split, grad_block, preferred_element_type=jnp.float32
        )
        dscores = (probs * (dprobs - delta_block[:, None, :])).astype(jnp.bfloat16)
        grad_key = grad_key + jnp.einsum(
            "hkq,qhd->hkd", dscores, query_block, preferred_element_type=jnp.float32
        )
        return (grad_key, grad_value)

    grad_key, grad_value = in_blocks(
        (
            lax.all_gather(query_rot, "seq", axis=0, tiled=True),
            lax.all_gather(grad_split, "seq", axis=0, tiled=True),
        ),
        (accum_init, accum_init),
        step,
    )

    def token_major(stack):
        return jnp.transpose(stack, (1, 0, 2))

    attended = token_major(output).reshape(rows, width).astype(jnp.bfloat16)
    grad_q = (
        rotate(token_major(grad_query), cosine, sine, -1.0)
        .reshape(rows, width)
        .astype(jnp.bfloat16)
    )
    grad_k = (
        rotate(token_major(grad_key) * scale, cosine, sine, -1.0)
        .reshape(rows, width)
        .astype(jnp.bfloat16)
    )
    grad_v = token_major(grad_value).reshape(rows, width).astype(jnp.bfloat16)
    return (attended, grad_q, grad_k, grad_v)


def solution(mesh):
    in_specs = (
        P(("seq", "head"), None),
        P(("seq", "head"), None),
        P(("seq", "head"), None),
        P(("seq", "head"), None),
        P(None, "seq"),
        P(),
        P(),
    )
    out_specs = (P("seq", "head"), P("seq", "head"), P("seq", "head"), P("seq", "head"))
    return jax.shard_map(
        on_device, mesh=mesh, in_specs=in_specs, out_specs=out_specs, check_vma=False
    )
```

profile of v0, /device:TPU:0, one launch (start us, length us, event | category | flops | bytes accessed | tf_op | source)
XLA Modules:
  0.0 208.3 jit_solution(673488734634136324)
XLA Ops:
  7.2 1.6 copy.97
  8.7 4.2 %all-to-all-start = ((bf16[32,4,512]{2,0,1:T(8,128)(2,1)}), bf16[32,4,512]{2,0,1:T(8,128)(2,1)S(1)}, u32[]{:S(2)}, u32[]{:S(2)}) async-start(bf16[32,4,512]{2,0,1:T(8,128)(2,1)} %bitcast.76), calls=%async_computation | async-start | bytes 262144 | tf_op jit(solution)/shard_map/all_to_all | solution.py:60
  13.0 0.8 convert_bitcast_fusion.4
  13.8 1.6 copy.96
  15.5 1.0 broadcast_multiply_fusion
  16.5 1.1 all-to-all-done
  17.6 3.3 %all-to-all-start.1 = ((bf16[32,4,512]{2,0,1:T(8,128)(2,1)}), bf16[32,4,512]{2,0,1:T(8,128)(2,1)S(1)}, u32[]{:S(2)}, u32[]{:S(2)}) async-start(bf16[32,4,512]{2,0,1:T(8,128)(2,1)} %bitcast.75), calls=%async_computation.1 | async-start | bytes 262144 | tf_op jit(solution)/shard_map/all_to_all | solution.py:61
  21.1 4.4 %all-to-all-done.1 = bf16[32,4,512]{2,0,1:T(8,128)(2,1)S(1)} async-done(((bf16[32,4,512]{2,0,1:T(8,128)(2,1)}), bf16[32,4,512]{2,0,1:T(8,128)(2,1)S(1)}, u32[]{:S(2)}, u32[]{:S(2)}) %all-to-all-start.1) | async-done | bytes 131104 | tf_op jit(solution)/shard_map/all_to_all | solution.py:61
  27.0 7.0 %all_to_all.58 = bf16[32,4,512]{2,0,1:T(8,128)(2,1)S(1)} all-to-all(bf16[32,4,512]{2,0,1:T(8,128)(2,1)S(1)} %bitcast.82), channel_id=1, replica_groups=mesh['seq'=8,'head'=4] {'head'}, dimensions={1} | all-to-all | bytes 262144 | tf_op jit(solution)/shard_map/all_to_all | solution.py:62
  36.4 3.3 %all-to-all-start.3 = ((bf16[32,4,512]{2,0,1:T(8,128)(2,1)}), bf16[32,4,512]{2,0,1:T(8,128)(2,1)S(1)}, u32[]{:S(2)}, u32[]{:S(2)}) async-start(bf16[32,4,512]{2,0,1:T(8,128)(2,1)} %bitcast.73), calls=%async_computation.3 | async-start | bytes 262144 | tf_op jit(solution)/shard_map/all_to_all | solution.py:63
  40.5 3.8 %all-to-all-done.3 = bf16[32,4,512]{2,0,1:T(8,128)(2,1)S(1)} async-done(((bf16[32,4,512]{2,0,1:T(8,128)(2,1)}), bf16[32,4,512]{2,0,1:T(8,128)(2,1)S(1)}, u32[]{:S(2)}, u32[]{:S(2)}) %all-to-all-start.3) | async-done | bytes 131104 | tf_op jit(solution)/shard_map/all_to_all | solution.py:63
  45.2 22.9 %all-gather.5.cloned.1.call-done = bf16[1024,4,128]{2,0,1:T(8,128)(2,1)} async-done(((bf16[128,4,128]{2,0,1:T(8,128)(2,1)}), bf16[1024,4,128]{2,0,1:T(8,128)(2,1)}) %all-gather.5.cloned.1.call-update) | async-done | bytes 1048592 | tf_op jit(solution)/shard_map/all_gather | solution.py:127
  68.2 1.9 fusion.31
  70.7 26.0 %all_gather.23 = f32[1024,4]{0,1:T(4,128)S(1)} all-gather(f32[128,4]{0,1:T(4,128)S(1)} %get-tuple-element.151), channel_id=1, replica_groups=mesh['seq'=8,'head'=4] {'seq'}, dimensions={0}, use_global_device_ids=true | all-gather | bytes 18432 | tf_op jit(solution)/shard_map/all_gather | solution.py:165
  96.7 12.5 %all-gather.7.cloned.1.call-done = bf16[1024,4,128]{0,2,1:T(8,128)(2,1)} async-done(((bf16[128,4,128]{0,2,1:T(8,128)(2,1)}), bf16[1024,4,128]{0,2,1:T(8,128)(2,1)}) %all-gather.7.cloned.1.call-update) | async-done | bytes 1048592 | tf_op jit(solution)/shard_map/all_gather | solution.py:128
  109.3 2.6 %multiply_reduce_fusion = (f32[128,4]{0,1:T(4,128)S(1)}, bf16[128,4,128]{0,2,1:T(8,128)(2,1)}) fusion(bf16[128,4,128]{0,2,1:T(8,128)(2,1)S(1)} %copy.51, f32[128,4]{0,1:T(4,128)S(1)} %get-tuple-element.152, bf16[1024,4,128]{0,2,1:T(8,128)(2,1)} %all-gather.7.cloned.1.call-done, f32[4,128,1024]{2,1,0:T(8,128)S(1)} %get-tuple-element.162, ...), kind=kOutput, calls=%fused_computation.34 | convolution fusion | flops 136183296 | bytes 3547136 | tf_op jit(solution)/shard_map/while/body/eval_jaxpr/hqk,khd->hqd/dot_general | solution.py:107
  111.9 26.0 %all_gather.25 = f32[1024,4]{0,1:T(4,128)S(1)} all-gather(f32[128,4]{0,1:T(4,128)S(1)} %get-tuple-element.125), channel_id=1, replica_groups=mesh['seq'=8,'head'=4] {'seq'}, dimensions={0}, use_global_device_ids=true | all-gather | bytes 18432 | tf_op jit(solution)/shard_map/all_gather | solution.py:166
  138.5 12.7 %all-gather.9.cloned.1.call-done = bf16[1024,4,128]{2,0,1:T(8,128)(2,1)} async-done(((bf16[128,4,128]{2,0,1:T(8,128)(2,1)}), bf16[1024,4,128]{2,0,1:T(8,128)(2,1)}) %all-gather.9.cloned.1.call-update) | async-done | bytes 1048592 | tf_op jit(solution)/shard_map/all_gather | solution.py:202
  151.1 1.9 exponential_select_fusion
  153.0 4.0 %fusion.9 = f32[128,4,128]{2,0,1:T(8,128)} fusion(bf16[1024,4,128]{2,0,1:T(8,128)(2,1)} %all-gather.5.cloned.1.call-done, f32[4,128,1024]{2,1,0:T(8,128)} %copy-done, bf16[1024,4,128]{0,2,1:T(8,128)(2,1)} %all-gather.7.cloned.1.call-done, f32[4,128]{1,0:T(4,128)} %bitcast.90, f32[4,128]{1,0:T(4,128)} %log_add_fusion, ...), kind=kOutput, calls=%fused_computation.15 | convolution fusion | flops 271122432 | bytes 4722688 | tf_op jit(solution)/shard_map/while/body/eval_jaxpr/hqk,khd->hqd/dot_general | solution.py:149
  157.1 35.6 %all-gather.11.cloned.1.call-done = bf16[1024,4,128]{2,0,1:T(8,128)(2,1)} async-done(((bf16[128,4,128]{2,0,1:T(8,128)(2,1)}), bf16[1024,4,128]{2,0,1:T(8,128)(2,1)}) %all-gather.11.cloned.1.call-update) | async-done | bytes 1048592 | tf_op jit(solution)/shard_map/all_gather | solution.py:203
  192.7 2.0 fusion.5
  194.7 2.0 subtract_convert_fusion
  197.8 1.0 pad_maximum_fusion.2
  (68 shorter events, 10.9 us)
Async XLA Ops:
  8.7 8.8 %all-to-all-start = ((bf16[32,4,512]{2,0,1:T(8,128)(2,1)}), bf16[32,4,512]{2,0,1:T(8,128)(2,1)S(1)}, u32[]{:S(2)}, u32[]{:S(2)}) async-start(bf16[32,4,512]{2,0,1:T(8,128)(2,1)} %bitcast.76), calls=%async_computation | async-start | bytes 262144 | tf_op jit(solution)/shard_map/all_to_all | solution.py:60
  16.5 9.5 %copy-start.5 = (f32[128,64]{1,0:T(8,128)}, f32[128,64]{1,0:T(8,128)S(1)}, u32[]{:S(2)}) copy-start(f32[128,64]{1,0:T(8,128)S(1)} %get-tuple-element.144) | copy-start | bytes 98308
  17.6 7.9 %all-to-all-start.1 = ((bf16[32,4,512]{2,0,1:T(8,128)(2,1)}), bf16[32,4,512]{2,0,1:T(8,128)(2,1)S(1)}, u32[]{:S(2)}, u32[]{:S(2)}) async-start(bf16[32,4,512]{2,0,1:T(8,128)(2,1)} %bitcast.75), calls=%async_computation.1 | async-start | bytes 262144 | tf_op jit(solution)/shard_map/all_to_all | solution.py:61
  20.9 47.3 %all-gather.5.cloned.1.call-start = ((), (), s32[]{:S(2)}) async-start(), calls=%async_computation.4 | async-start | bytes 1179648 | tf_op jit(solution)/shard_map/all_gather | solution.py:127
  25.6 1.4 copy-start.6
  26.0 9.8 %copy-start.7 = (bf16[32,2048]{1,0:T(8,128)(2,1)S(1)}, bf16[32,2048]{1,0:T(8,128)(2,1)}, u32[]{:S(2)}) copy-start(bf16[32,2048]{1,0:T(8,128)(2,1)} %param.10) | copy-start | bytes 393220
  26.0 13.8 %copy-start.9 = (s32[1024]{0:T(1024)S(1)}, s32[1024]{0:T(1024)}, u32[]{:S(2)}) copy-start(s32[1024]{0:T(1024)} %param.12) | copy-start | bytes 12292
  26.0 13.9 %copy-start.11 = (s32[6,2]{0,1:T(2,128)S(1)}, s32[6,2]{0,1:T(2,128)}, u32[]{:S(2)}) copy-start(s32[6,2]{0,1:T(2,128)} %param.13) | copy-start | bytes 148
  27.0 82.3 %all-gather.7.cloned.1.call-start = ((), (), s32[]{:S(2)}) async-start(), calls=%async_computation.5 | async-start | bytes 1179648 | tf_op jit(solution)/shard_map/all_gather | solution.py:128
  34.9 116.2 %all-gather.9.cloned.1.call-start = ((), (), s32[]{:S(2)}) async-start(), calls=%async_computation.6 | async-start | bytes 1179648 | tf_op jit(solution)/shard_map/all_gather | solution.py:202
  36.4 7.9 %all-to-all-start.3 = ((bf16[32,4,512]{2,0,1:T(8,128)(2,1)}), bf16[32,4,512]{2,0,1:T(8,128)(2,1)S(1)}, u32[]{:S(2)}, u32[]{:S(2)}) async-start(bf16[32,4,512]{2,0,1:T(8,128)(2,1)} %bitcast.73), calls=%async_computation.3 | async-start | bytes 262144 | tf_op jit(solution)/shard_map/all_to_all | solution.py:63
  39.8 153.0 %all-gather.11.cloned.1.call-start = ((), (), s32[]{:S(2)}) async-start(), calls=%async_computation.7 | async-start | bytes 1179648 | tf_op jit(solution)/shard_map/all_gather | solution.py:203
  70.1 41.8 %copy-start = (f32[4,128,1024]{2,1,0:T(8,128)}, f32[4,128,1024]{2,1,0:T(8,128)S(1)}, u32[]{:S(2)}) copy-start(f32[4,128,1024]{2,1,0:T(8,128)S(1)} %get-tuple-element.162) | copy-start | bytes 6291460
  109.3 41.9 %copy-start.4 = (bf16[128,4,128]{2,0,1:T(8,128)(2,1)S(1)}, bf16[128,4,128]{2,0,1:T(8,128)(2,1)}, u32[]{:S(2)}) copy-start(bf16[128,4,128]{2,0,1:T(8,128)(2,1)} %pad_maximum_fusion.1) | copy-start | bytes 393220
  111.9 41.2 %copy-start.10 = (f32[128,4]{0,1:T(4,128)}, f32[128,4]{0,1:T(4,128)S(1)}, u32[]{:S(2)}) copy-start(f32[128,4]{0,1:T(4,128)S(1)} %get-tuple-element.125) | copy-start | bytes 6148
  153.0 39.7 %copy-start.2 = (bf16[1024,4,128]{2,0,1:T(8,128)(2,1)S(1)}, bf16[1024,4,128]{2,0,1:T(8,128)(2,1)}, u32[]{:S(2)}) copy-start(bf16[1024,4,128]{2,0,1:T(8,128)(2,1)} %all-gather.9.cloned.1.call-done) | copy-start | bytes 3145732
  153.0 39.7 %copy-start.3 = (bf16[128,4,128]{0,2,1:T(8,128)(2,1)S(1)}, bf16[128,4,128]{0,2,1:T(8,128)(2,1)}, u32[]{:S(2)}) copy-start(bf16[128,4,128]{0,2,1:T(8,128)(2,1)} %copy.47) | copy-start | bytes 393220
  194.7 5.0 %copy-start.1 = (bf16[1024,4,128]{2,0,1:T(8,128)(2,1)S(1)}, bf16[1024,4,128]{2,0,1:T(8,128)(2,1)}, u32[]{:S(2)}) copy-start(bf16[1024,4,128]{2,0,1:T(8,128)(2,1)} %all-gather.11.cloned.1.call-done) | copy-start | bytes 3145732
  198.8 2.2 %copy-start.8 = (bf16[128,4,128]{0,2,1:T(8,128)(2,1)S(1)}, bf16[128,4,128]{0,2,1:T(8,128)(2,1)}, u32[]{:S(2)}) copy-start(bf16[128,4,128]{0,2,1:T(8,128)(2,1)} %get-tuple-element.126) | copy-start | bytes 393220
Sparse Core Ops, SparseCore 0:
  27.1 41.0 all-gather.4
  70.8 38.4 all-gather.6
  112.0 39.0 all-gather.8
  153.7 38.9 all-gather.10
where the time goes:
time: 209 us; the launch traced here: 208 us
  waiting for transfers between devices  93.2 us (45%)
  blocking collectives  59.1 us (28%)
  between operations  14 us (7%)
  matrix products  12.9 us (6%)
  starting transfers between devices  11 us (5%)
  local copies, waits for them, and re-layouts  9.49 us (5%)
  other arithmetic  8.62 us (4%)
    all_gather x1, waiting for transfers between devices, on_device(): lax.all_gather(grad_split, 'seq', axis=0, tiled=True)  35.6 us
    all_gather x1, blocking collectives, on_device(): lax.all_gather(level.T, 'seq', axis=0, tiled=True)  26 us
    all_gather x1, blocking collectives, on_device(): lax.all_gather(delta.T, 'seq', axis=0, tiled=True)  26 us
    all_gather x1, waiting for transfers between devices, on_device(): lax.all_gather(key_rot, 'seq', axis=0, tiled=True)  22.9 us
    all_gather x1, waiting for transfers between devices, on_device(): lax.all_gather(query_rot, 'seq', axis=0, tiled=True)  12.7 us
    all_gather x1, waiting for transfers between devices, on_device(): lax.all_gather(value_split, 'seq', axis=0, tiled=True)  12.5 us
    all_to_all x1, blocking collectives, on_device(): lax.all_to_all(v_in, 'head', split_axis=1, concat_axis=0, tiled=True)  7.02 us
    all_to_all x1, waiting for transfers between devices, on_device(): lax.all_to_all(k_in, 'head', split_axis=1, concat_axis=0, tiled=True)  4.42 us
  transfers between devices with their start and end apart: 7, of which 7 were waited for; matrix products, arithmetic and copies ran while one was open for 9% of the time, Pallas kernels for 0%

commit v1 on v0

--- a/solution.py
+++ b/solution.py
@@ -1,6 +1,12 @@
+import functools
+import math
+
 import jax
 import jax.numpy as jnp
+import numpy as np
 from jax import lax
+from jax.experimental import pallas as pl
+from jax.experimental.pallas import tpu as pltpu
 from jax.sharding import PartitionSpec as P
 
 HD = 128
@@ -224,7 +230,296 @@
     return (attended, grad_q, grad_k, grad_v)
 
 
+LOG2E = math.log2(math.e)
+VMEM_LIMIT = 48 * 1024 * 1024
+PAD = 3
+
+
+def whole(space=pltpu.VMEM):
+    return pl.BlockSpec(memory_space=space)
+
+
+def inverse_steps():
+    side = HD // 6 * 2
+    first = HD - 2 * side
+    parts, rows = [], []
+    for row, group in ((0, first), (1, side), (2, side)):
+        steps = np.arange(group // 2, dtype=np.float64)
+        parts.append(THETA ** (-2.0 * steps / group))
+        rows.append(np.full(group // 2, row))
+    table = np.zeros((HD // 2, 8), np.float32)
+    table[np.arange(HD // 2), np.concatenate(rows)] = np.concatenate(parts)
+    return table
+
+
+def prepare_kernel(row_first, head_of, pos_ref, step_ref, q_ref, k_ref, v_ref, g_ref, out_ref, table_ref):
+    rows = q_ref.shape[0]
+    angle = (
+        step_ref[:, 0:1] * pos_ref[0:1, :].astype(jnp.float32)
+        + step_ref[:, 1:2] * pos_ref[1:2, :].astype(jnp.float32)
+        + step_ref[:, 2:3] * pos_ref[2:3, :].astype(jnp.float32)
+    )
+    cosine, sine = jnp.cos(angle), jnp.sin(angle)
+    table_ref[0] = jnp.concatenate([cosine, cosine], axis=0).T
+    table_ref[1] = jnp.concatenate([-sine, sine], axis=0).T
+    own = pl.ds(pl.multiple_of(row_first() * rows, rows), rows)
+    cosine, sine = table_ref[0, own, :], table_ref[1, own, :]
+    for chip, head in enumerate(head_of):
+        lanes = slice(head * HD, (head + 1) * HD)
+        for at, ref in ((0, q_ref), (1, k_ref)):
+            x = ref[:, lanes].astype(jnp.float32)
+            out_ref[chip, at * rows : (at + 1) * rows, :] = (
+                x * cosine + pltpu.roll(x, HD // 2, 1) * sine
+            ).astype(jnp.bfloat16)
+        out_ref[chip, 2 * rows : 3 * rows, :] = v_ref[:, lanes]
+        out_ref[chip, 3 * rows : 4 * rows, :] = g_ref[:, lanes]
+
+
+def attend_kernel(
+    core_of, views_ref, near_ref, mine_ref, other_ref, out_ref,
+    q_all, g_all, k_all, v_all, kt_all, vt_all, s_all, d_all, p_all, ds_all, dk_all, dv_all, order, rank,
+):
+    blocks = out_ref.shape[0]
+    half = out_ref.shape[1] // 4
+    rows = half // 2
+    block = 2 * half
+    count = near_ref.shape[0]
+    span = count_span(count, blocks)
+    wide = 2 * block
+    core = core_of()
+    scale = HD**-0.5
+    first, held = [], []
+    for view in range(count):
+        below, equal = 0, 0
+        for b in range(blocks):
+            below = below + (views_ref[b * block] < view).astype(jnp.int32)
+            equal = equal + (views_ref[b * block] == view).astype(jnp.int32)
+        first.append(below)
+        held.append(equal)
+
+    def pick(table, at):
+        value = table[0]
+        for view in range(1, count):
+            value = jnp.where(at == view, table[view], value)
+        return value
+
+    last, now, place = jnp.int32(0), near_ref[0, 0], jnp.int32(0)
+    start, size = [], []
+    cycle = [last, now]
+    for _ in range(count - 2):
+        one, two = near_ref[now, 0], near_ref[now, 1]
+        last, now = now, jnp.where(one == last, two, one)
+        cycle.append(now)
+    for i, view in enumerate(cycle):
+        f, n = pick(first, view), pick(held, view)
+        start.append(place)
+        size.append(n)
+        for extra in range(2):
+            order[place + extra] = f + extra
+            rank[place + extra] = jnp.int32(i)
+        place = place + n
+    for pos in range(blocks):
+        src = order[pos]
+        spots = [pos + PAD]
+        if pos - blocks + PAD >= 0:
+            spots.append(pos - blocks + PAD)
+        if pos + blocks + PAD < blocks + 2 * PAD:
+            spots.append(pos + blocks + PAD)
+
+        def take(at):
+            part = slice(at * rows, (at + 1) * rows)
+            return jnp.concatenate(
+                [mine_ref[2 * src, part, :], mine_ref[2 * src + 1, part, :],
+                 other_ref[2 * src, part, :], other_ref[2 * src + 1, part, :]], axis=0)
+
+        tile, at = pos // 2, pos % 2
+        for ref, source in ((q_all, take(0)), (g_all, take(3))):
+            base = tile * wide + at * half
+            ref[base : base + half, :] = source[:half]
+            ref[base + block : base + block + half, :] = source[half:]
+        for ref, turned, source in ((k_all, kt_all, take(1)), (v_all, vt_all, take(2))):
+            across = source.astype(jnp.float32).T.astype(jnp.bfloat16)
+            for spot in spots:
+                ref[spot * block : (spot + 1) * block, :] = source
+                if turned is kt_all:
+                    turned[:, spot * block : (spot + 1) * block] = across
+                else:
+                    turned[:, spot * block : (spot + 1) * block] = across
+    dk_all[...] = jnp.zeros_like(dk_all)
+    dv_all[...] = jnp.zeros_like(dv_all)
+
+    nt = (((1,), (1,)), ((), ()))
+    lane = lax.broadcasted_iota(jnp.int32, (1, wide), 1)
+    second = (lane // half) % 2 == 1
+
+    for tile in range(blocks // 2):
+        rank_a, rank_b = rank[2 * tile], rank[2 * tile + 1]
+        before = lax.rem(rank_a + count - 1, count)
+        begin = pick(start, rank_a) - pick(size, before) + PAD
+        window = pl.ds(pl.multiple_of(begin * block, block), span * block)
+        q_tile = q_all[tile * wide : (tile + 1) * wide, :]
+        g_tile = g_all[tile * wide : (tile + 1) * wide, :]
+        s_all[...] = lax.dot_general(k_all[window, :], q_tile, nt, preferred_element_type=jnp.float32)
+        d_all[...] = lax.dot_general(v_all[window, :], g_tile, nt, preferred_element_type=jnp.float32)
+        top = jnp.full((1, wide), NEG, jnp.float32)
+        oks = []
+        for i in range(span):
+            at = lax.rem(begin - PAD + i + blocks, blocks)
+            key_rank = rank[at]
+            far_a = lax.rem(key_rank - rank_a + count, count)
+            far_b = lax.rem(key_rank - rank_b + count, count)
+            ok_a = ((far_a <= 1) | (far_a == count - 1)).astype(jnp.int32)
+            ok_b = ((far_b <= 1) | (far_b == count - 1)).astype(jnp.int32)
+            ok = jnp.where(second, ok_b, ok_a) > 0
+            oks.append(ok)
+            part = jnp.where(ok, s_all[i * block : (i + 1) * block, :], NEG)
+            top = jnp.maximum(top, jnp.max(part, axis=0, keepdims=True))
+        factor = scale * LOG2E
+        level = top * factor
+        total = jnp.zeros((1, wide), jnp.float32)
+        delta = jnp.zeros((1, wide), jnp.float32)
+        for i in range(span):
+            here = slice(i * block, (i + 1) * block)
+            e = jnp.where(oks[i], jnp.exp2(s_all[here, :] * factor - level), 0.0)
+            s_all[here, :] = e
+            total = total + jnp.sum(e, axis=0, keepdims=True)
+            delta = delta + jnp.sum(e * d_all[here, :], axis=0, keepdims=True)
+            ds_all[here, :] = e.astype(jnp.bfloat16)
+        share = 1.0 / total
+        delta = delta * share
+        out_t = jnp.dot(vt_all[:, window], ds_all[:, :block], preferred_element_type=jnp.float32)
+        out = (out_t * share[:, :block]).T.astype(jnp.bfloat16)
+        for i in range(span):
+            here = slice(i * block, (i + 1) * block)
+            p = s_all[here, :] * share
+            p_all[i, :, :] = p[:half].astype(jnp.bfloat16)
+            ds_all[here, :] = (p * (d_all[here, :] - delta)).astype(jnp.bfloat16)
+        dq_t = jnp.dot(kt_all[:, window], ds_all[:, :block], preferred_element_type=jnp.float32)
+        dq = (dq_t * scale).T.astype(jnp.bfloat16)
+        own = pl.ds(pl.multiple_of(begin * half, half), span * half)
+        dv_all[own, :] += jnp.dot(p_all[...].reshape(span * half, wide), g_tile, preferred_element_type=jnp.float32)
+        mine_ds = ds_all[...].reshape(span, block, wide)[:, :half].reshape(span * half, wide)
+        dk_all[own, :] += jnp.dot(mine_ds, q_tile, preferred_element_type=jnp.float32)
+        for at in range(2):
+            src = order[2 * tile + at]
+            to = src // 2 + (blocks // 2) * (lax.rem(src, 2) != core).astype(jnp.int32)
+            out_ref[to, 0:half, :] = out[at * half : (at + 1) * half]
+            out_ref[to, half : 2 * half, :] = dq[at * half : (at + 1) * half]
+    for pos in range(blocks):
+        src = order[pos]
+        to = src // 2 + (blocks // 2) * (lax.rem(src, 2) != core).astype(jnp.int32)
+        spots = [pos + PAD]
+        if pos - blocks + PAD >= 0:
+            spots.append(pos - blocks + PAD)
+        if pos + blocks + PAD < blocks + 2 * PAD:
+            spots.append(pos + blocks + PAD)
+        dk = sum(dk_all[spot * half : (spot + 1) * half, :] for spot in spots)
+        dv = sum(dv_all[spot * half : (spot + 1) * half, :] for spot in spots)
+        out_ref[to, 2 * half : 3 * half, :] = (dk * scale).astype(jnp.bfloat16)
+        out_ref[to, 3 * half : 4 * half, :] = dv.astype(jnp.bfloat16)
+
+
+def finish_kernel(core_of, table_ref, keep_ref, swap_ref, att_ref, dq_ref, dk_ref, dv_ref):
+    heads = swap_ref.shape[0]
+    half = keep_ref.shape[1] // 4
+    rows = half // 2
+    core = core_of()
+    for ref, which in ((keep_ref, core), (swap_ref, 1 - core)):
+        for pair in range(2):
+            there = pl.ds(pl.multiple_of(pair * half + which * rows, rows), rows)
+            cosine, sine = table_ref[0, there, :], table_ref[1, there, :]
+            for head in range(heads):
+                lanes = slice(head * HD, (head + 1) * HD)
+                for at, out in ((0, att_ref), (1, dq_ref), (2, dk_ref), (3, dv_ref)):
+                    x = ref[head, at * half + pair * rows : at * half + (pair + 1) * rows, :]
+                    if at in (1, 2):
+                        x = x.astype(jnp.float32)
+                        x = x * cosine - pltpu.roll(x, HD // 2, 1) * sine
+                        x = x.astype(jnp.bfloat16)
+                    out[there, lanes] = x
+
+
+def count_span(count, blocks):
+    return 4 + blocks - count
+
+
+def by_chip(seqs, parts, q_in, k_in, v_in, grad_out, positions, views, adjacency):
+    rows, width = q_in.shape
+    heads = width // HD
+    xs = parts // 2
+    group = heads // parts
+    chips = seqs * xs
+    block = rows * parts
+    half = block // 2
+    count = adjacency.shape[0]
+    span = count_span(count, seqs)
+    long = seqs + 2 * PAD
+    wide = 2 * block
+    head_of = [((c % xs) * 2 + (c // xs) % 2) * group + c // xs // 2 for c in range(chips)]
+    limits = pltpu.CompilerParams(vmem_limit_bytes=VMEM_LIMIT)
+
+    def row_first():
+        return lax.axis_index("head")
+
+    def core_of():
+        return lax.rem(lax.axis_index("head"), 2)
+
+    sent, table = pl.pallas_call(
+        functools.partial(prepare_kernel, row_first, head_of),
+        out_shape=(
+            jax.ShapeDtypeStruct((chips, 4 * rows, HD), jnp.bfloat16),
+            jax.ShapeDtypeStruct((2, block, HD), jnp.float32),
+        ),
+        in_specs=[whole()] * 6,
+        out_specs=(whole(), whole()),
+        compiler_params=limits,
+        name="prepare",
+    )(positions, jnp.asarray(inverse_steps()), q_in, k_in, v_in, grad_out)
+    axes = ("seq", "head")
+    same_core = [[(c // xs) * parts + (c % xs) * 2 + core for c in range(chips)] for core in range(2)]
+    mine = lax.all_to_all(sent, axes, 0, 0, axis_index_groups=same_core, tiled=True)
+    partner = [(d, d ^ 1) for d in range(seqs * parts)]
+    other = lax.ppermute(mine, axes, partner)
+    back = pl.pallas_call(
+        functools.partial(attend_kernel, core_of),
+        out_shape=jax.ShapeDtypeStruct((seqs, 4 * half, HD), jnp.bfloat16),
+        in_specs=[whole(pltpu.SMEM), whole(pltpu.SMEM), whole(), whole()],
+        out_specs=whole(),
+        scratch_shapes=[
+            pltpu.VMEM((seqs * block, HD), jnp.bfloat16),
+            pltpu.VMEM((seqs * block, HD), jnp.bfloat16),
+            pltpu.VMEM((long * block, HD), jnp.bfloat16),
+            pltpu.VMEM((long * block, HD), jnp.bfloat16),
+            pltpu.VMEM((HD, long * block), jnp.bfloat16),
+            pltpu.VMEM((HD, long * block), jnp.bfloat16),
+            pltpu.VMEM((span * block, wide), jnp.float32),
+            pltpu.VMEM((span * block, wide), jnp.float32),
+            pltpu.VMEM((span, half, wide), jnp.bfloat16),
+            pltpu.VMEM((span * block, wide), jnp.bfloat16),
+            pltpu.VMEM((long * half, HD), jnp.float32),
+            pltpu.VMEM((long * half, HD), jnp.float32),
+            pltpu.SMEM((seqs + 1,), jnp.int32),
+            pltpu.SMEM((seqs + 1,), jnp.int32),
+        ],
+        compiler_params=limits,
+        name="attend",
+    )(views, adjacency, mine, other)
+    ranked = [[s for s in range(seqs) if s % 2 == core] + [s for s in range(seqs) if s % 2 != core] for core in range(2)]
+    along = [[s * parts + x * 2 + core for s in ranked[core]] for x in range(xs) for core in range(2)]
+    keep = lax.all_to_all(back, axes, 0, 0, axis_index_groups=along, tiled=True)
+    swap = lax.ppermute(keep[seqs // 2 :], axes, partner)
+    return pl.pallas_call(
+        functools.partial(finish_kernel, core_of),
+        out_shape=(jax.ShapeDtypeStruct((block, group * HD), jnp.bfloat16),) * 4,
+        in_specs=[whole()] * 3,
+        out_specs=(whole(),) * 4,
+        compiler_params=limits,
+        name="finish",
+    )(table, keep, swap)
+
+
 def solution(mesh):
+    seqs, parts = mesh.shape["seq"], mesh.shape["head"]
     in_specs = (
         P(("seq", "head"), None),
         P(("seq", "head"), None),
@@ -235,6 +530,20 @@
         P(),
     )
     out_specs = (P("seq", "head"), P("seq", "head"), P("seq", "head"), P("seq", "head"))
-    return jax.shard_map(
-        on_device, mesh=mesh, in_specs=in_specs, out_specs=out_specs, check_vma=False
-    )
+
+    def run(*args):
+        heads = args[0].shape[1] // HD
+        count = args[6].shape[0]
+        fits = (
+            seqs * parts == 2 * heads
+            and seqs % 2 == 0
+            and parts % 2 == 0
+            and count <= seqs < 2 * count
+            and count_span(count, seqs) <= seqs
+        )
+        step = functools.partial(by_chip, seqs, parts) if fits else on_device
+        return jax.shard_map(
+            step, mesh=mesh, in_specs=in_specs, out_specs=out_specs, check_vma=False
+        )(*args)
+
+    return run

time: 209 us -> 57.7 us (0.28)
  waiting for transfers between devices: 93.2 us -> 3.33 us
  blocking collectives: 59.1 us -> 41.6 us
  between operations: 14 us -> 0.69 us
  matrix products: 12.9 us -> 0 us
  starting transfers between devices: 11 us -> 0.07 us
  other arithmetic: 8.62 us -> 0 us
  Pallas kernels: 0 us -> 6.52 us
  local copies, waits for them, and re-layouts: 9.49 us -> 5.17 us
    all_gather x4 -> x0, waiting for transfers between devices: 83.7 us -> none  [the longest x1 35.6 us: on_device(): lax.all_gather(grad_split, 'seq', axis=0, tiled=True)]
    all_gather x2 -> x0, blocking collectives: 52 us -> none  [the longest x1 26 us: on_device(): lax.all_gather(level.T, 'seq', axis=0, tiled=True)]
    all_to_all x1 -> x2, blocking collectives: 7.02 us -> 41.6 us  [the longest x1 23.2 us: by_chip(): lax.all_to_all(sent, axes, 0, 0, axis_index_groups=same_core, tiled=True)]
    dot_general x6 -> x0, matrix products: 12.9 us -> none  [the longest x1 4.04 us: step(): jnp.einsum('hqk,khd->hqd', dscores, key_block, preferred_element_type=jnp...]
    all_to_all x3 -> x0, starting transfers between devices: 10.9 us -> none  [the longest x1 4.21 us: on_device(): lax.all_to_all(q_in, 'head', split_axis=1, concat_axis=0, tiled=True)]
    all_to_all x3 -> x0, waiting for transfers between devices: 9.35 us -> none  [the longest x1 4.42 us: on_device(): lax.all_to_all(k_in, 'head', split_axis=1, concat_axis=0, tiled=True)]
    pallas_call x0 -> x3, Pallas kernels: none -> 6.52 us  [the longest x1 5.21 us: by_chip(): pl.pallas_call(functools.partial(attend_kernel, core_of), out_shape=jax.S...]
    all_to_all x4 -> x0, local copies, waits for them, and re-layouts: 3.81 us -> none  [the longest x1 1.57 us: on_device(): lax.all_to_all(q_in, 'head', split_axis=1, concat_axis=0, tiled=True)]
  transfers between devices with their start and end apart: 7 -> 2, of which waited for: 7 -> 2; matrix products, arithmetic and copies ran while one was open for 9% -> 0% of each run, Pallas kernels for 0% -> 0%
where the time goes in v1:
time: 57.7 us; the launch traced here: 57.4 us
  blocking collectives  41.6 us (72%)
  Pallas kernels  6.52 us (11%)
  local copies, waits for them, and re-layouts  5.17 us (9%)
  waiting for transfers between devices  3.33 us (6%)
  between operations  0.69 us (1%)
    all_to_all x1, blocking collectives, by_chip(): lax.all_to_all(sent, axes, 0, 0, axis_index_groups=same_core, tiled=True)  23.2 us
    all_to_all x1, blocking collectives, by_chip(): keep = lax.all_to_all(back, axes, 0, 0, axis_index_groups=along, tiled=True)  18.4 us
    pallas_call x1, Pallas kernels, by_chip(): pl.pallas_call(functools.partial(attend_kernel, core_of), out_shape=jax.S...  5.21 us
    unnamed x17, local copies, waits for them, and re-layouts  5.15 us
    ppermute x1, waiting for transfers between devices, by_chip(): other = lax.ppermute(mine, axes, partner)  1.81 us
    ppermute x1, waiting for transfers between devices, by_chip(): swap = lax.ppermute(keep[seqs // 2:], axes, partner)  1.52 us
  transfers between devices with their start and end apart: 2, of which 2 were waited for; matrix products, arithmetic and copies ran while one was open for 0% of the time, Pallas kernels for 0%

profile of v1, /device:TPU:0, one launch (start us, length us, event | category | flops | bytes accessed | tf_op | source)
XLA Modules:
  0.0 57.4 jit_solution(16305746940971525032)
XLA Ops:
  0.6 0.0 copy-start
  0.6 0.9 %copy-done = bf16[32,2048]{1,0:T(8,128)(2,1)S(1)} copy-done((bf16[32,2048]{1,0:T(8,128)(2,1)S(1)}, bf16[32,2048]{1,0:T(8,128)(2,1)}, u32[]{:S(2)}) %copy-start) | copy-done | bytes 131096
  1.5 0.0 copy-start.1
  1.5 0.9 %copy-done.1 = bf16[32,2048]{1,0:T(8,128)(2,1)S(1)} copy-done((bf16[32,2048]{1,0:T(8,128)(2,1)S(1)}, bf16[32,2048]{1,0:T(8,128)(2,1)}, u32[]{:S(2)}) %copy-start.1) | copy-done | bytes 131096
  2.4 0.0 copy-start.2
  2.4 0.9 %copy-done.2 = bf16[32,2048]{1,0:T(8,128)(2,1)S(1)} copy-done((bf16[32,2048]{1,0:T(8,128)(2,1)S(1)}, bf16[32,2048]{1,0:T(8,128)(2,1)}, u32[]{:S(2)}) %copy-start.2) | copy-done | bytes 131096
  3.3 0.0 copy-start.3
  3.3 0.9 %copy-done.3 = bf16[32,2048]{1,0:T(8,128)(2,1)S(1)} copy-done((bf16[32,2048]{1,0:T(8,128)(2,1)S(1)}, bf16[32,2048]{1,0:T(8,128)(2,1)}, u32[]{:S(2)}) %copy-start.3) | copy-done | bytes 131096
  4.3 0.0 copy-start.4
  4.3 0.8 %copy-done.4 = f32[64,8]{1,0:T(8,128)S(1)} copy-done((f32[64,8]{1,0:T(8,128)S(1)}, f32[64,8]{1,0:T(8,128)}, u32[]{:S(2)}) %copy-start.4) | copy-done | bytes 2072
  5.0 0.7 %copy-done.6 = s32[3,128]{1,0:T(4,128)S(1)} copy-done((s32[3,128]{1,0:T(4,128)S(1)}, s32[3,128]{1,0:T(4,128)}, u32[]{:S(2)}) %copy-start.6) | copy-done | bytes 1560
  5.7 0.4 prepare.1
  6.1 0.0 copy-start.7
  6.1 23.2 %all_to_all.10.mine_ref = bf16[16,128,128]{2,1,0:T(8,128)(2,1)S(1)} all-to-all(bf16[16,128,128]{2,1,0:T(8,128)(2,1)S(1)} %get-tuple-element.7), channel_id=1, replica_groups={{0,2,4,6,8,10,12,14,16,18,20,22,24,26,28,30},{1,3,5,7,9,11,13,15,17,19,..., dimensions={0} | all-to-all | bytes 1048576 | tf_op jit(solution)/shard_map/all_to_all | solution.py:480
  29.4 0.0 collective-permute-start
  29.4 0.0 copy-done.7
  29.4 0.1 copy.12.near_ref
  29.5 1.8 %collective-permute-done.other_ref = bf16[16,128,128]{2,1,0:T(8,128)(2,1)S(1)} collective-permute-done((bf16[16,128,128]{2,1,0:T(8,128)(2,1)S(1)}, bf16[16,128,128]{2,1,0:T(8,128)(2,1)S(1)}, u32[]{:S(2)}, u32[]{:S(2)}) %collective-permute-start) | collective-permute-done | bytes 524320 | tf_op jit(solution)/shard_map/ppermute | solution.py:482
  31.3 0.0 copy-done.5
  31.3 5.2 %attend.1 = bf16[8,256,128]{2,1,0:T(8,128)(2,1)S(1)} custom-call(s32[1024]{0:T(1024)S(1)} %copy-done.5, s32[6,2]{1,0:T(8,128)S(1)} %copy.12.near_ref, bf16[16,128,128]{2,1,0:T(8,128)(2,1)S(1)} %all_to_all.10.mine_ref, bf16[16,128,128]{2,1,0:T(8,128)(2,1)S(1)} %collective-permute-done.other_ref), custom_call_target="tpu_custom_call" | custom-call | tf_op jit(solution)/shard_map/attend/pallas_call | solution.py:483
  36.5 18.4 %all_to_all.11.keep_ref = bf16[8,256,128]{2,1,0:T(8,128)(2,1)S(1)} all-to-all(bf16[8,256,128]{2,1,0:T(8,128)(2,1)S(1)} %attend.1), channel_id=1, replica_groups={{0,8,16,24,4,12,20,28},{5,13,21,29,1,9,17,25},{2,10,18,26,6,14,22,30},{..., dimensions={0} | all-to-all | bytes 1048576 | tf_op jit(solution)/shard_map/all_to_all | solution.py:509
  54.9 0.1 collective-permute-start.1
  55.0 1.5 %collective-permute-done.1.swap_ref = bf16[4,256,128]{2,1,0:T(8,128)(2,1)S(1)} collective-permute-done((bf16[4,256,128]{2,1,0:T(8,128)(2,1)S(1)}, bf16[4,256,128]{2,1,0:T(8,128)(2,1)S(1)}, u32[]{:S(2)}, u32[]{:S(2)}) %collective-permute-start.1) | collective-permute-done | bytes 262176 | tf_op jit(solution)/shard_map/ppermute | solution.py:510
  56.5 0.9 %finish.1 = (bf16[128,512]{1,0:T(8,128)(2,1)}, bf16[128,512]{1,0:T(8,128)(2,1)}, bf16[128,512]{1,0:T(8,128)(2,1)}, bf16[128,512]{1,0:T(8,128)(2,1)}) custom-call(f32[2,128,128]{2,1,0:T(8,128)S(1)} %get-tuple-element.6.table_ref, bf16[8,256,128]{2,1,0:T(8,128)(2,1)S(1)} %all_to_all.11.keep_ref, bf16[4,256,128]{2,1,0:T(8,128)(2,1)S(1)} %collective-permute-done.1.swap_ref), custom_call_target="tpu_custom_call" | custom-call | tf_op jit(solution)/shard_map/finish/pallas_call | solution.py:511
  (3 shorter events, 0.0 us)
Async XLA Ops:
  0.6 0.9 %copy-start = (bf16[32,2048]{1,0:T(8,128)(2,1)S(1)}, bf16[32,2048]{1,0:T(8,128)(2,1)}, u32[]{:S(2)}) copy-start(bf16[32,2048]{1,0:T(8,128)(2,1)} %q_ref.1) | copy-start | bytes 393220
  1.5 0.9 %copy-start.1 = (bf16[32,2048]{1,0:T(8,128)(2,1)S(1)}, bf16[32,2048]{1,0:T(8,128)(2,1)}, u32[]{:S(2)}) copy-start(bf16[32,2048]{1,0:T(8,128)(2,1)} %k_ref.1) | copy-start | bytes 393220
  2.4 0.9 %copy-start.2 = (bf16[32,2048]{1,0:T(8,128)(2,1)S(1)}, bf16[32,2048]{1,0:T(8,128)(2,1)}, u32[]{:S(2)}) copy-start(bf16[32,2048]{1,0:T(8,128)(2,1)} %v_ref.1) | copy-start | bytes 393220
  3.3 0.9 %copy-start.3 = (bf16[32,2048]{1,0:T(8,128)(2,1)S(1)}, bf16[32,2048]{1,0:T(8,128)(2,1)}, u32[]{:S(2)}) copy-start(bf16[32,2048]{1,0:T(8,128)(2,1)} %g_ref.1) | copy-start | bytes 393220
  4.3 0.8 %copy-start.4 = (f32[64,8]{1,0:T(8,128)S(1)}, f32[64,8]{1,0:T(8,128)}, u32[]{:S(2)}) copy-start(f32[64,8]{1,0:T(8,128)} %constant.2.clone.step_ref) | copy-start | bytes 6148
  5.0 0.7 %copy-start.6 = (s32[3,128]{1,0:T(4,128)S(1)}, s32[3,128]{1,0:T(4,128)}, u32[]{:S(2)}) copy-start(s32[3,128]{1,0:T(4,128)} %pos_ref.1) | copy-start | bytes 4612
  6.1 23.3 %copy-start.7 = (s32[6,2]{0,1:T(2,128)S(1)}, s32[6,2]{0,1:T(2,128)}, u32[]{:S(2)}) copy-start(s32[6,2]{0,1:T(2,128)} %param.14) | copy-start | bytes 148
  29.4 1.9 %copy-start.5 = (s32[1024]{0:T(1024)S(1)}, s32[1024]{0:T(1024)}, u32[]{:S(2)}) copy-start(s32[1024]{0:T(1024)} %views_ref.1) | copy-start | bytes 12292
  29.4 1.9 %collective-permute-start = (bf16[16,128,128]{2,1,0:T(8,128)(2,1)S(1)}, bf16[16,128,128]{2,1,0:T(8,128)(2,1)S(1)}, u32[]{:S(2)}, u32[]{:S(2)}) collective-permute-start(bf16[16,128,128]{2,1,0:T(8,128)(2,1)S(1)} %all_to_all.10.mine_ref), channel_id=1, source_target_pairs={{0,1},{1,0},{2,3},{3,2},{4,5},{5,4},{6,7},{7,6},{8,9},{9,8},{10,11... | collective-permute-start | bytes 1572872 | tf_op jit(solution)/shard_map/ppermute | solution.py:482
  54.9 1.6 %collective-permute-start.1 = (bf16[4,256,128]{2,1,0:T(8,128)(2,1)S(1)}, bf16[4,256,128]{2,1,0:T(8,128)(2,1)S(1)}, u32[]{:S(2)}, u32[]{:S(2)}) collective-permute-start(bf16[4,256,128]{2,1,0:T(8,128)(2,1)S(1)} %slice.4), channel_id=1, source_target_pairs={{0,1},{1,0},{2,3},{3,2},{4,5},{5,4},{6,7},{7,6},{8,9},{9,8},{10,11... | collective-permute-start | bytes 786440 | tf_op jit(solution)/shard_map/ppermute | solution.py:510

commit v2 on v1

--- a/solution.py
+++ b/solution.py
@@ -252,8 +252,19 @@
     return table
 
 
-def prepare_kernel(row_first, head_of, pos_ref, step_ref, q_ref, k_ref, v_ref, g_ref, out_ref, table_ref):
+def prepare_kernel(
+    row_first, head_of, pos_hbm, step_hbm, q_hbm, k_hbm, v_hbm, g_hbm, out_ref, table_ref,
+    pos_ref, step_ref, q_ref, k_ref, v_ref, g_ref, sems,
+):
     rows = q_ref.shape[0]
+    pairs = (
+        (pos_hbm, pos_ref), (step_hbm, step_ref), (q_hbm, q_ref), (k_hbm, k_ref), (v_hbm, v_ref), (g_hbm, g_ref)
+    )
+    copies = [pltpu.make_async_copy(src, dst, sems.at[i]) for i, (src, dst) in enumerate(pairs)]
+    for copy in copies:
+        copy.start()
+    copies[0].wait()
+    copies[1].wait()
     angle = (
         step_ref[:, 0:1] * pos_ref[0:1, :].astype(jnp.float32)
         + step_ref[:, 1:2] * pos_ref[1:2, :].astype(jnp.float32)
@@ -264,6 +275,8 @@
     table_ref[1] = jnp.concatenate([-sine, sine], axis=0).T
     own = pl.ds(pl.multiple_of(row_first() * rows, rows), rows)
     cosine, sine = table_ref[0, own, :], table_ref[1, own, :]
+    for copy in copies[2:]:
+        copy.wait()
     for chip, head in enumerate(head_of):
         lanes = slice(head * HD, (head + 1) * HD)
         for at, ref in ((0, q_ref), (1, k_ref)):
@@ -276,17 +289,16 @@
 
 
 def attend_kernel(
-    core_of, views_ref, near_ref, mine_ref, other_ref, out_ref,
+    core_of, slab_of, views_ref, near_ref, mine_ref, other_ref, out_ref,
     q_all, g_all, k_all, v_all, kt_all, vt_all, s_all, d_all, p_all, ds_all, dk_all, dv_all, order, rank,
 ):
-    blocks = out_ref.shape[0]
-    half = out_ref.shape[1] // 4
-    rows = half // 2
-    block = 2 * half
+    blocks = mine_ref.shape[0] // 2
+    rows = mine_ref.shape[1] // 4
+    block = 4 * rows
     count = near_ref.shape[0]
     span = count_span(count, blocks)
     wide = 2 * block
-    core = core_of()
+    core, slab = core_of(), slab_of()
     scale = HD**-0.5
     first, held = [], []
     for view in range(count):
@@ -318,39 +330,39 @@
             order[place + extra] = f + extra
             rank[place + extra] = jnp.int32(i)
         place = place + n
+
+    def spots(pos):
+        at = [pos + PAD]
+        if pos - blocks + PAD >= 0:
+            at.append(pos - blocks + PAD)
+        if pos + blocks < blocks + PAD:
+            at.append(pos + blocks + PAD)
+        return at
+
     for pos in range(blocks):
         src = order[pos]
-        spots = [pos + PAD]
-        if pos - blocks + PAD >= 0:
-            spots.append(pos - blocks + PAD)
-        if pos + blocks + PAD < blocks + 2 * PAD:
-            spots.append(pos + blocks + PAD)
-
-        def take(at):
+        base = (pos + PAD) * block
+        for at, ref, base in (
+            (0, q_all, pos * block), (1, k_all, base), (2, v_all, base), (3, g_all, pos * block)
+        ):
             part = slice(at * rows, (at + 1) * rows)
-            return jnp.concatenate(
-                [mine_ref[2 * src, part, :], mine_ref[2 * src + 1, part, :],
-                 other_ref[2 * src, part, :], other_ref[2 * src + 1, part, :]], axis=0)
-
-        tile, at = pos // 2, pos % 2
-        for ref, source in ((q_all, take(0)), (g_all, take(3))):
-            base = tile * wide + at * half
-            ref[base : base + half, :] = source[:half]
-            ref[base + block : base + block + half, :] = source[half:]
-        for ref, turned, source in ((k_all, kt_all, take(1)), (v_all, vt_all, take(2))):
+            for x in range(2):
+                for whose, c in ((mine_ref, core), (other_ref, 1 - core)):
+                    to = pl.ds(pl.multiple_of(base + (2 * x + c) * rows, rows), rows)
+                    ref[to, :] = whose[2 * src + x, part, :]
+        for ref, turned in ((k_all, kt_all), (v_all, vt_all)):
+            source = ref[(pos + PAD) * block : (pos + PAD + 1) * block, :]
             across = source.astype(jnp.float32).T.astype(jnp.bfloat16)
-            for spot in spots:
-                ref[spot * block : (spot + 1) * block, :] = source
-                if turned is kt_all:
-                    turned[:, spot * block : (spot + 1) * block] = across
-                else:
-                    turned[:, spot * block : (spot + 1) * block] = across
+            for n, spot in enumerate(spots(pos)):
+                if n:
+                    ref[spot * block : (spot + 1) * block, :] = source
+                turned[:, spot * block : (spot + 1) * block] = across
     dk_all[...] = jnp.zeros_like(dk_all)
     dv_all[...] = jnp.zeros_like(dv_all)
 
     nt = (((1,), (1,)), ((), ()))
     lane = lax.broadcasted_iota(jnp.int32, (1, wide), 1)
-    second = (lane // half) % 2 == 1
+    second = lane >= block
 
     for tile in range(blocks // 2):
         rank_a, rank_b = rank[2 * tile], rank[2 * tile + 1]
@@ -365,9 +377,8 @@
         oks = []
         for i in range(span):
             at = lax.rem(begin - PAD + i + blocks, blocks)
-            key_rank = rank[at]
-            far_a = lax.rem(key_rank - rank_a + count, count)
-            far_b = lax.rem(key_rank - rank_b + count, count)
+            far_a = lax.rem(rank[at] - rank_a + count, count)
+            far_b = lax.rem(rank[at] - rank_b + count, count)
             ok_a = ((far_a <= 1) | (far_a == count - 1)).astype(jnp.int32)
             ok_b = ((far_b <= 1) | (far_b == count - 1)).astype(jnp.int32)
             ok = jnp.where(second, ok_b, ok_a) > 0
@@ -387,56 +398,49 @@
             ds_all[here, :] = e.astype(jnp.bfloat16)
         share = 1.0 / total
         delta = delta * share
-        out_t = jnp.dot(vt_all[:, window], ds_all[:, :block], preferred_element_type=jnp.float32)
-        out = (out_t * share[:, :block]).T.astype(jnp.bfloat16)
+        out_t = jnp.dot(vt_all[:, window], ds_all[...], preferred_element_type=jnp.float32) * share
         for i in range(span):
             here = slice(i * block, (i + 1) * block)
             p = s_all[here, :] * share
-            p_all[i, :, :] = p[:half].astype(jnp.bfloat16)
+            p_all[here, :] = p.astype(jnp.bfloat16)
             ds_all[here, :] = (p * (d_all[here, :] - delta)).astype(jnp.bfloat16)
-        dq_t = jnp.dot(kt_all[:, window], ds_all[:, :block], preferred_element_type=jnp.float32)
-        dq = (dq_t * scale).T.astype(jnp.bfloat16)
-        own = pl.ds(pl.multiple_of(begin * half, half), span * half)
-        dv_all[own, :] += jnp.dot(p_all[...].reshape(span * half, wide), g_tile, preferred_element_type=jnp.float32)
-        mine_ds = ds_all[...].reshape(span, block, wide)[:, :half].reshape(span * half, wide)
-        dk_all[own, :] += jnp.dot(mine_ds, q_tile, preferred_element_type=jnp.float32)
+        dq_t = jnp.dot(kt_all[:, window], ds_all[...], preferred_element_type=jnp.float32) * scale
+        dv_all[window, :] += jnp.dot(p_all[...], g_tile, preferred_element_type=jnp.float32)
+        dk_all[window, :] += jnp.dot(ds_all[...], q_tile, preferred_element_type=jnp.float32)
         for at in range(2):
             src = order[2 * tile + at]
-            to = src // 2 + (blocks // 2) * (lax.rem(src, 2) != core).astype(jnp.int32)
-            out_ref[to, 0:half, :] = out[at * half : (at + 1) * half]
-            out_ref[to, half : 2 * half, :] = dq[at * half : (at + 1) * half]
+
+            @pl.when(lax.rem(src, 2) == core)
+            def _():
+                to = jnp.bitwise_xor(src // 2, slab)
+                out_ref[to, 0] = out_t[:, at * block : (at + 1) * block].T.astype(jnp.bfloat16)
+                out_ref[to, 1] = dq_t[:, at * block : (at + 1) * block].T.astype(jnp.bfloat16)
+
     for pos in range(blocks):
         src = order[pos]
-        to = src // 2 + (blocks // 2) * (lax.rem(src, 2) != core).astype(jnp.int32)
-        spots = [pos + PAD]
-        if pos - blocks + PAD >= 0:
-            spots.append(pos - blocks + PAD)
-        if pos + blocks + PAD < blocks + 2 * PAD:
-            spots.append(pos + blocks + PAD)
-        dk = sum(dk_all[spot * half : (spot + 1) * half, :] for spot in spots)
-        dv = sum(dv_all[spot * half : (spot + 1) * half, :] for spot in spots)
-        out_ref[to, 2 * half : 3 * half, :] = (dk * scale).astype(jnp.bfloat16)
-        out_ref[to, 3 * half : 4 * half, :] = dv.astype(jnp.bfloat16)
-
-
-def finish_kernel(core_of, table_ref, keep_ref, swap_ref, att_ref, dq_ref, dk_ref, dv_ref):
-    heads = swap_ref.shape[0]
-    half = keep_ref.shape[1] // 4
-    rows = half // 2
-    core = core_of()
-    for ref, which in ((keep_ref, core), (swap_ref, 1 - core)):
-        for pair in range(2):
-            there = pl.ds(pl.multiple_of(pair * half + which * rows, rows), rows)
-            cosine, sine = table_ref[0, there, :], table_ref[1, there, :]
-            for head in range(heads):
-                lanes = slice(head * HD, (head + 1) * HD)
-                for at, out in ((0, att_ref), (1, dq_ref), (2, dk_ref), (3, dv_ref)):
-                    x = ref[head, at * half + pair * rows : at * half + (pair + 1) * rows, :]
-                    if at in (1, 2):
-                        x = x.astype(jnp.float32)
-                        x = x * cosine - pltpu.roll(x, HD // 2, 1) * sine
-                        x = x.astype(jnp.bfloat16)
-                    out[there, lanes] = x
+
+        @pl.when(lax.rem(src, 2) == core)
+        def _():
+            to = jnp.bitwise_xor(src // 2, slab)
+            dk = sum(dk_all[spot * block : (spot + 1) * block, :] for spot in spots(pos))
+            dv = sum(dv_all[spot * block : (spot + 1) * block, :] for spot in spots(pos))
+            out_ref[to, 2] = (dk * scale).astype(jnp.bfloat16)
+            out_ref[to, 3] = dv.astype(jnp.bfloat16)
+
+
+def finish_kernel(slab_of, table_ref, *refs):
+    chunks, outs = refs[:-4], refs[-4:]
+    slab = slab_of()
+    cosine, sine = table_ref[0], table_ref[1]
+    for m, ref in enumerate(chunks):
+        lanes = pl.ds(pl.multiple_of(jnp.bitwise_xor(slab, m) * HD, HD), HD)
+        for at, out in enumerate(outs):
+            x = ref[at]
+            if at in (1, 2):
+                x = x.astype(jnp.float32)
+                x = x * cosine - pltpu.roll(x, HD // 2, 1) * sine
+                x = x.astype(jnp.bfloat16)
+            out[:, lanes] = x
 
 
 def count_span(count, blocks):
@@ -445,14 +449,11 @@
 
 def by_chip(seqs, parts, q_in, k_in, v_in, grad_out, positions, views, adjacency):
     rows, width = q_in.shape
-    heads = width // HD
     xs = parts // 2
-    group = heads // parts
+    group = width // HD // parts
     chips = seqs * xs
     block = rows * parts
-    half = block // 2
-    count = adjacency.shape[0]
-    span = count_span(count, seqs)
+    span = count_span(adjacency.shape[0], seqs)
     long = seqs + 2 * PAD
     wide = 2 * block
     head_of = [((c % xs) * 2 + (c // xs) % 2) * group + c // xs // 2 for c in range(chips)]
@@ -464,25 +465,34 @@
     def core_of():
         return lax.rem(lax.axis_index("head"), 2)
 
+    def slab_of():
+        return lax.axis_index("seq") // 2
+
+    steps = inverse_steps()
     sent, table = pl.pallas_call(
         functools.partial(prepare_kernel, row_first, head_of),
         out_shape=(
             jax.ShapeDtypeStruct((chips, 4 * rows, HD), jnp.bfloat16),
             jax.ShapeDtypeStruct((2, block, HD), jnp.float32),
         ),
-        in_specs=[whole()] * 6,
+        in_specs=[whole(pltpu.HBM)] * 6,
         out_specs=(whole(), whole()),
+        scratch_shapes=[
+            pltpu.VMEM(positions.shape, jnp.int32),
+            pltpu.VMEM(steps.shape, jnp.float32),
+            *[pltpu.VMEM((rows, width), jnp.bfloat16)] * 4,
+            pltpu.SemaphoreType.DMA((6,)),
+        ],
         compiler_params=limits,
         name="prepare",
-    )(positions, jnp.asarray(inverse_steps()), q_in, k_in, v_in, grad_out)
+    )(positions, jnp.asarray(steps), q_in, k_in, v_in, grad_out)
     axes = ("seq", "head")
     same_core = [[(c // xs) * parts + (c % xs) * 2 + core for c in range(chips)] for core in range(2)]
     mine = lax.all_to_all(sent, axes, 0, 0, axis_index_groups=same_core, tiled=True)
-    partner = [(d, d ^ 1) for d in range(seqs * parts)]
-    other = lax.ppermute(mine, axes, partner)
+    other = lax.ppermute(mine, axes, [(d, d ^ 1) for d in range(seqs * parts)])
     back = pl.pallas_call(
-        functools.partial(attend_kernel, core_of),
-        out_shape=jax.ShapeDtypeStruct((seqs, 4 * half, HD), jnp.bfloat16),
+        functools.partial(attend_kernel, core_of, slab_of),
+        out_shape=jax.ShapeDtypeStruct((group, 4, block, HD), jnp.bfloat16),
         in_specs=[whole(pltpu.SMEM), whole(pltpu.SMEM), whole(), whole()],
         out_specs=whole(),
         scratch_shapes=[
@@ -494,28 +504,34 @@
             pltpu.VMEM((HD, long * block), jnp.bfloat16),
             pltpu.VMEM((span * block, wide), jnp.float32),
             pltpu.VMEM((span * block, wide), jnp.float32),
-            pltpu.VMEM((span, half, wide), jnp.bfloat16),
             pltpu.VMEM((span * block, wide), jnp.bfloat16),
-            pltpu.VMEM((long * half, HD), jnp.float32),
-            pltpu.VMEM((long * half, HD), jnp.float32),
+            pltpu.VMEM((span * block, wide), jnp.bfloat16),
+            pltpu.VMEM((long * block, HD), jnp.float32),
+            pltpu.VMEM((long * block, HD), jnp.float32),
             pltpu.SMEM((seqs + 1,), jnp.int32),
             pltpu.SMEM((seqs + 1,), jnp.int32),
         ],
         compiler_params=limits,
         name="attend",
     )(views, adjacency, mine, other)
-    ranked = [[s for s in range(seqs) if s % 2 == core] + [s for s in range(seqs) if s % 2 != core] for core in range(2)]
-    along = [[s * parts + x * 2 + core for s in ranked[core]] for x in range(xs) for core in range(2)]
-    keep = lax.all_to_all(back, axes, 0, 0, axis_index_groups=along, tiled=True)
-    swap = lax.ppermute(keep[seqs // 2 :], axes, partner)
+
+    def route(m):
+        pairs = []
+        for d in range(seqs * parts):
+            s, h = divmod(d, parts)
+            to_s = ((s // 2) ^ m) * 2 + h % 2
+            pairs.append((d, to_s * parts + h // 2 * 2 + s % 2))
+        return pairs
+
+    chunks = {m: lax.ppermute(back[m], axes, route(m)) for m in reversed(range(group))}
     return pl.pallas_call(
-        functools.partial(finish_kernel, core_of),
+        functools.partial(finish_kernel, slab_of),
         out_shape=(jax.ShapeDtypeStruct((block, group * HD), jnp.bfloat16),) * 4,
-        in_specs=[whole()] * 3,
+        in_specs=[whole()] * (1 + group),
         out_specs=(whole(),) * 4,
         compiler_params=limits,
         name="finish",
-    )(table, keep, swap)
+    )(table, *[chunks[m] for m in range(group)])
 
 
 def solution(mesh):
@@ -538,6 +554,7 @@
             seqs * parts == 2 * heads
             and seqs % 2 == 0
             and parts % 2 == 0
+            and seqs & (seqs - 1) == 0
             and count <= seqs < 2 * count
             and count_span(count, seqs) <= seqs
         )

time: 57.7 us -> 55 us (0.953)
  blocking collectives: 41.6 us -> 23.3 us
  waiting for transfers between devices: 3.33 us -> 12 us
  starting transfers between devices: 0.07 us -> 5.11 us
  Pallas kernels: 6.52 us -> 8.39 us
    all_to_all x1 -> x0, blocking collectives: 18.4 us -> none  [by_chip(): keep = lax.all_to_all(back, axes, 0, 0, axis_index_groups=along, tiled=True)]
    ppermute x2 -> x5, waiting for transfers between devices: 3.33 us -> 12 us  [the longest x4 10.2 us: by_chip(): lax.ppermute(back[m], axes, route(m))]
    ppermute x2 -> x5, starting transfers between devices: 0.07 us -> 5.11 us  [the longest x4 5.11 us: by_chip(): lax.ppermute(back[m], axes, route(m))]
    pallas_call x2, Pallas kernels: 6.09 us -> 7.15 us  [the longest x1 6.24 us: by_chip(): pl.pallas_call(functools.partial(attend_kernel, core_of, slab_of), out_sh...]
    pallas_call x1, Pallas kernels: 0.43 us -> 1.23 us  [by_chip(): pl.pallas_call(functools.partial(prepare_kernel, row_first, head_of), out...]
  transfers between devices with their start and end apart: 2 -> 5, of which waited for: 2 -> 3; matrix products, arithmetic and copies ran while one was open for 0% -> 0% of each run, Pallas kernels for 0% -> 0%
where the time goes in v2:
time: 55 us; the launch traced here: 54.7 us
  blocking collectives  23.3 us (42%)
  waiting for transfers between devices  12 us (22%)
  Pallas kernels  8.39 us (15%)
  local copies, waits for them, and re-layouts  5.19 us (9%)
  starting transfers between devices  5.11 us (9%)
  between operations  0.7 us (1%)
    all_to_all x1, blocking collectives, by_chip(): lax.all_to_all(sent, axes, 0, 0, axis_index_groups=same_core, tiled=True)  23.3 us
    ppermute x4, waiting for transfers between devices, by_chip(): lax.ppermute(back[m], axes, route(m))  10.2 us
    pallas_call x1, Pallas kernels, by_chip(): pl.pallas_call(functools.partial(attend_kernel, core_of, slab_of), out_sh...  6.24 us
    unnamed x17, local copies, waits for them, and re-layouts  5.15 us
    ppermute x4, starting transfers between devices, by_chip(): lax.ppermute(back[m], axes, route(m))  5.11 us
    ppermute x1, waiting for transfers between devices, by_chip(): other = lax.ppermute(mine, axes, [(d, d ^ 1) for d in range(seqs * parts)])  1.81 us
    pallas_call x1, Pallas kernels, by_chip(): pl.pallas_call(functools.partial(prepare_kernel, row_first, head_of), out...  1.23 us
  transfers between devices with their start and end apart: 5, of which 3 were waited for; matrix products, arithmetic and copies ran while one was open for 0% of the time, Pallas kernels for 0%

profile of v2, /device:TPU:0, one launch (start us, length us, event | category | flops | bytes accessed | tf_op | source)
XLA Modules:
  0.0 54.7 jit_solution(13702713198318500522)
XLA Ops:
  0.6 0.0 copy-start
  0.6 0.9 %copy-done = bf16[32,2048]{1,0:T(8,128)(2,1)S(1)} copy-done((bf16[32,2048]{1,0:T(8,128)(2,1)S(1)}, bf16[32,2048]{1,0:T(8,128)(2,1)}, u32[]{:S(2)}) %copy-start) | copy-done | bytes 131096
  1.5 0.9 %copy-done.1 = bf16[32,2048]{1,0:T(8,128)(2,1)S(1)} copy-done((bf16[32,2048]{1,0:T(8,128)(2,1)S(1)}, bf16[32,2048]{1,0:T(8,128)(2,1)}, u32[]{:S(2)}) %copy-start.1) | copy-done | bytes 131096
  2.4 0.9 %copy-done.2 = bf16[32,2048]{1,0:T(8,128)(2,1)S(1)} copy-done((bf16[32,2048]{1,0:T(8,128)(2,1)S(1)}, bf16[32,2048]{1,0:T(8,128)(2,1)}, u32[]{:S(2)}) %copy-start.2) | copy-done | bytes 131096
  3.3 0.9 %copy-done.3 = bf16[32,2048]{1,0:T(8,128)(2,1)S(1)} copy-done((bf16[32,2048]{1,0:T(8,128)(2,1)S(1)}, bf16[32,2048]{1,0:T(8,128)(2,1)}, u32[]{:S(2)}) %copy-start.3) | copy-done | bytes 131096
  4.3 0.8 %copy-done.4 = f32[64,8]{1,0:T(8,128)S(1)} copy-done((f32[64,8]{1,0:T(8,128)S(1)}, f32[64,8]{1,0:T(8,128)}, u32[]{:S(2)}) %copy-start.4) | copy-done | bytes 2072
  5.0 0.7 %copy-done.6 = s32[3,128]{1,0:T(4,128)S(1)} copy-done((s32[3,128]{1,0:T(4,128)S(1)}, s32[3,128]{1,0:T(4,128)}, u32[]{:S(2)}) %copy-start.6) | copy-done | bytes 1560
  5.7 1.2 %prepare.1 = (bf16[16,128,128]{2,1,0:T(8,128)(2,1)S(1)}, f32[2,128,128]{2,1,0:T(8,128)S(1)}) custom-call(s32[3,128]{1,0:T(4,128)S(1)} %copy-done.6, f32[64,8]{1,0:T(8,128)S(1)} %copy-done.4, bf16[32,2048]{1,0:T(8,128)(2,1)S(1)} %copy-done, bf16[32,2048]{1,0:T(8,128)(2,1)S(1)} %copy-done.1, bf16[32,2048]{1,0:T(8,128)(2,1)S(1)} %copy-done.2, ...), custom_call_target="tpu_custom_call" | custom-call | tf_op jit(solution)/shard_map/prepare/pallas_call | solution.py:472
  6.9 0.0 copy-start.7
  6.9 23.3 %all_to_all.5.mine_ref = bf16[16,128,128]{2,1,0:T(8,128)(2,1)S(1)} all-to-all(bf16[16,128,128]{2,1,0:T(8,128)(2,1)S(1)} %get-tuple-element.7), channel_id=1, replica_groups={{0,2,4,6,8,10,12,14,16,18,20,22,24,26,28,30},{1,3,5,7,9,11,13,15,17,19,..., dimensions={0} | all-to-all | bytes 1048576 | tf_op jit(solution)/shard_map/all_to_all | solution.py:491
  30.2 0.0 collective-permute-start
  30.2 0.1 copy.12.near_ref
  30.3 1.8 %collective-permute-done.other_ref = bf16[16,128,128]{2,1,0:T(8,128)(2,1)S(1)} collective-permute-done((bf16[16,128,128]{2,1,0:T(8,128)(2,1)S(1)}, bf16[16,128,128]{2,1,0:T(8,128)(2,1)S(1)}, u32[]{:S(2)}, u32[]{:S(2)}) %collective-permute-start) | collective-permute-done | bytes 524320 | tf_op jit(solution)/shard_map/ppermute | solution.py:492
  32.1 0.0 copy-done.5
  32.1 6.2 %attend.1 = bf16[4,4,128,128]{3,2,1,0:T(8,128)(2,1)S(1)} custom-call(s32[1024]{0:T(1024)S(1)} %copy-done.5, s32[6,2]{1,0:T(8,128)S(1)} %copy.12.near_ref, bf16[16,128,128]{2,1,0:T(8,128)(2,1)S(1)} %all_to_all.5.mine_ref, bf16[16,128,128]{2,1,0:T(8,128)(2,1)S(1)} %collective-permute-done.other_ref), custom_call_target="tpu_custom_call" | custom-call | tf_op jit(solution)/shard_map/attend/pallas_call | solution.py:493
  38.4 1.7 %collective-permute-start.4 = (bf16[4,128,128]{2,1,0:T(8,128)(2,1)S(1)}, bf16[4,128,128]{2,1,0:T(8,128)(2,1)S(1)}, u32[]{:S(2)}, u32[]{:S(2)}) collective-permute-start(bf16[4,128,128]{2,1,0:T(8,128)(2,1)S(1)} %get-tuple-element.8), channel_id=1, source_target_pairs={{0,24},{1,28},{2,26},{3,30},{4,25},{5,29},{6,27},{7,31},{8,16},{9,... | collective-permute-start | bytes 393224 | tf_op jit(solution)/shard_map/ppermute | solution.py:526
  40.1 1.1 %collective-permute-start.3 = (bf16[4,128,128]{2,1,0:T(8,128)(2,1)S(1)}, bf16[4,128,128]{2,1,0:T(8,128)(2,1)S(1)}, u32[]{:S(2)}, u32[]{:S(2)}) collective-permute-start(bf16[4,128,128]{2,1,0:T(8,128)(2,1)S(1)} %get-tuple-element.9), channel_id=1, source_target_pairs={{0,16},{1,20},{2,18},{3,22},{4,17},{5,21},{6,19},{7,23},{8,24},{9,... | collective-permute-start | bytes 393224 | tf_op jit(solution)/shard_map/ppermute | solution.py:526
  41.2 1.7 %collective-permute-start.2 = (bf16[4,128,128]{2,1,0:T(8,128)(2,1)S(1)}, bf16[4,128,128]{2,1,0:T(8,128)(2,1)S(1)}, u32[]{:S(2)}, u32[]{:S(2)}) collective-permute-start(bf16[4,128,128]{2,1,0:T(8,128)(2,1)S(1)} %get-tuple-element.10), channel_id=1, source_target_pairs={{0,8},{1,12},{2,10},{3,14},{4,9},{5,13},{6,11},{7,15},{8,0},{9,4},... | collective-permute-start | bytes 393224 | tf_op jit(solution)/shard_map/ppermute | solution.py:526
  42.9 0.7 %collective-permute-start.1 = (bf16[4,128,128]{2,1,0:T(8,128)(2,1)S(1)}, bf16[4,128,128]{2,1,0:T(8,128)(2,1)S(1)}, u32[]{:S(2)}, u32[]{:S(2)}) collective-permute-start(bf16[4,128,128]{2,1,0:T(8,128)(2,1)S(1)} %get-tuple-element.11), channel_id=1, source_target_pairs={{0,0},{1,4},{2,2},{3,6},{4,1},{5,5},{6,3},{7,7},{8,8},{9,12},{10,1... | collective-permute-start | bytes 393224 | tf_op jit(solution)/shard_map/ppermute | solution.py:526
  43.5 3.2 %collective-permute-done.4.refs_3_ = bf16[4,128,128]{2,1,0:T(8,128)(2,1)S(1)} collective-permute-done((bf16[4,128,128]{2,1,0:T(8,128)(2,1)S(1)}, bf16[4,128,128]{2,1,0:T(8,128)(2,1)S(1)}, u32[]{:S(2)}, u32[]{:S(2)}) %collective-permute-start.4) | collective-permute-done | bytes 131104 | tf_op jit(solution)/shard_map/ppermute | solution.py:526
  46.7 7.0 %collective-permute-done.3.refs_2_ = bf16[4,128,128]{2,1,0:T(8,128)(2,1)S(1)} collective-permute-done((bf16[4,128,128]{2,1,0:T(8,128)(2,1)S(1)}, bf16[4,128,128]{2,1,0:T(8,128)(2,1)S(1)}, u32[]{:S(2)}, u32[]{:S(2)}) %collective-permute-start.3) | collective-permute-done | bytes 131104 | tf_op jit(solution)/shard_map/ppermute | solution.py:526
  53.8 0.0 collective-permute-done.2.refs_1_
  53.8 0.0 collective-permute-done.1.refs_0_
  53.8 0.9 %finish.1 = (bf16[128,512]{1,0:T(8,128)(2,1)}, bf16[128,512]{1,0:T(8,128)(2,1)}, bf16[128,512]{1,0:T(8,128)(2,1)}, bf16[128,512]{1,0:T(8,128)(2,1)}) custom-call(f32[2,128,128]{2,1,0:T(8,128)S(1)} %get-tuple-element.6.table_ref, bf16[4,128,128]{2,1,0:T(8,128)(2,1)S(1)} %collective-permute-done.1.refs_0_, ...), custom_call_target="tpu_custom_call" | custom-call | tf_op jit(solution)/shard_map/finish/pallas_call | solution.py:527
  (8 shorter events, 0.0 us)
Async XLA Ops:
  0.6 0.9 %copy-start = (bf16[32,2048]{1,0:T(8,128)(2,1)S(1)}, bf16[32,2048]{1,0:T(8,128)(2,1)}, u32[]{:S(2)}) copy-start(bf16[32,2048]{1,0:T(8,128)(2,1)} %q_hbm.1) | copy-start | bytes 393220
  1.5 0.9 %copy-start.1 = (bf16[32,2048]{1,0:T(8,128)(2,1)S(1)}, bf16[32,2048]{1,0:T(8,128)(2,1)}, u32[]{:S(2)}) copy-start(bf16[32,2048]{1,0:T(8,128)(2,1)} %k_hbm.1) | copy-start | bytes 393220
  2.4 0.9 %copy-start.2 = (bf16[32,2048]{1,0:T(8,128)(2,1)S(1)}, bf16[32,2048]{1,0:T(8,128)(2,1)}, u32[]{:S(2)}) copy-start(bf16[32,2048]{1,0:T(8,128)(2,1)} %v_hbm.1) | copy-start | bytes 393220
  3.3 0.9 %copy-start.3 = (bf16[32,2048]{1,0:T(8,128)(2,1)S(1)}, bf16[32,2048]{1,0:T(8,128)(2,1)}, u32[]{:S(2)}) copy-start(bf16[32,2048]{1,0:T(8,128)(2,1)} %g_hbm.1) | copy-start | bytes 393220
  4.3 0.8 %copy-start.4 = (f32[64,8]{1,0:T(8,128)S(1)}, f32[64,8]{1,0:T(8,128)}, u32[]{:S(2)}) copy-start(f32[64,8]{1,0:T(8,128)} %constant.2.clone.step_hbm) | copy-start | bytes 6148
  5.0 0.7 %copy-start.6 = (s32[3,128]{1,0:T(4,128)S(1)}, s32[3,128]{1,0:T(4,128)}, u32[]{:S(2)}) copy-start(s32[3,128]{1,0:T(4,128)} %pos_hbm.1) | copy-start | bytes 4612
  6.9 23.3 %copy-start.7 = (s32[6,2]{0,1:T(2,128)S(1)}, s32[6,2]{0,1:T(2,128)}, u32[]{:S(2)}) copy-start(s32[6,2]{0,1:T(2,128)} %param.14) | copy-start | bytes 148
  30.2 1.9 %copy-start.5 = (s32[1024]{0:T(1024)S(1)}, s32[1024]{0:T(1024)}, u32[]{:S(2)}) copy-start(s32[1024]{0:T(1024)} %views_ref.1) | copy-start | bytes 12292
  30.2 1.9 %collective-permute-start = (bf16[16,128,128]{2,1,0:T(8,128)(2,1)S(1)}, bf16[16,128,128]{2,1,0:T(8,128)(2,1)S(1)}, u32[]{:S(2)}, u32[]{:S(2)}) collective-permute-start(bf16[16,128,128]{2,1,0:T(8,128)(2,1)S(1)} %all_to_all.5.mine_ref), channel_id=1, source_target_pairs={{0,1},{1,0},{2,3},{3,2},{4,5},{5,4},{6,7},{7,6},{8,9},{9,8},{10,11... | collective-permute-start | bytes 1572872 | tf_op jit(solution)/shard_map/ppermute | solution.py:492
  38.4 8.3 %collective-permute-start.4 = (bf16[4,128,128]{2,1,0:T(8,128)(2,1)S(1)}, bf16[4,128,128]{2,1,0:T(8,128)(2,1)S(1)}, u32[]{:S(2)}, u32[]{:S(2)}) collective-permute-start(bf16[4,128,128]{2,1,0:T(8,128)(2,1)S(1)} %get-tuple-element.8), channel_id=1, source_target_pairs={{0,24},{1,28},{2,26},{3,30},{4,25},{5,29},{6,27},{7,31},{8,16},{9,... | collective-permute-start | bytes 393224 | tf_op jit(solution)/shard_map/ppermute | solution.py:526
  40.1 13.7 %collective-permute-start.3 = (bf16[4,128,128]{2,1,0:T(8,128)(2,1)S(1)}, bf16[4,128,128]{2,1,0:T(8,128)(2,1)S(1)}, u32[]{:S(2)}, u32[]{:S(2)}) collective-permute-start(bf16[4,128,128]{2,1,0:T(8,128)(2,1)S(1)} %get-tuple-element.9), channel_id=1, source_target_pairs={{0,16},{1,20},{2,18},{3,22},{4,17},{5,21},{6,19},{7,23},{8,24},{9,... | collective-permute-start | bytes 393224 | tf_op jit(solution)/shard_map/ppermute | solution.py:526
  41.2 12.5 %collective-permute-start.2 = (bf16[4,128,128]{2,1,0:T(8,128)(2,1)S(1)}, bf16[4,128,128]{2,1,0:T(8,128)(2,1)S(1)}, u32[]{:S(2)}, u32[]{:S(2)}) collective-permute-start(bf16[4,128,128]{2,1,0:T(8,128)(2,1)S(1)} %get-tuple-element.10), channel_id=1, source_target_pairs={{0,8},{1,12},{2,10},{3,14},{4,9},{5,13},{6,11},{7,15},{8,0},{9,4},... | collective-permute-start | bytes 393224 | tf_op jit(solution)/shard_map/ppermute | solution.py:526
  42.9 10.9 %collective-permute-start.1 = (bf16[4,128,128]{2,1,0:T(8,128)(2,1)S(1)}, bf16[4,128,128]{2,1,0:T(8,128)(2,1)S(1)}, u32[]{:S(2)}, u32[]{:S(2)}) collective-permute-start(bf16[4,128,128]{2,1,0:T(8,128)(2,1)S(1)} %get-tuple-element.11), channel_id=1, source_target_pairs={{0,0},{1,4},{2,2},{3,6},{4,1},{5,5},{6,3},{7,7},{8,8},{9,12},{10,1... | collective-permute-start | bytes 393224 | tf_op jit(solution)/shard_map/ppermute | solution.py:526

commit v3 on v2

--- a/solution.py
+++ b/solution.py
@@ -483,7 +483,7 @@
             *[pltpu.VMEM((rows, width), jnp.bfloat16)] * 4,
             pltpu.SemaphoreType.DMA((6,)),
         ],
-        compiler_params=limits,
+        compiler_params=pltpu.CompilerParams(vmem_limit_bytes=60*1024*1024),
         name="prepare",
     )(positions, jnp.asarray(steps), q_in, k_in, v_in, grad_out)
     axes = ("seq", "head")

time: 55 us -> 51 us (0.927)
  local copies, waits for them, and re-layouts: 5.19 us -> 0.15 us
  Pallas kernels: 8.39 us -> 9.31 us
    unnamed x17 -> x7, local copies, waits for them, and re-layouts: 5.15 us -> 0.11 us
    pallas_call x1, Pallas kernels: 1.23 us -> 2.15 us  [by_chip(): pl.pallas_call(functools.partial(prepare_kernel, row_first, head_of), out...]
where the time goes in v3:
time: 51 us; the launch traced here: 50.8 us
  blocking collectives  23.5 us (46%)
  waiting for transfers between devices  12 us (24%)
  Pallas kernels  9.31 us (18%)
  starting transfers between devices  5.11 us (10%)
  between operations  0.69 us (1%)
    all_to_all x1, blocking collectives, by_chip(): lax.all_to_all(sent, axes, 0, 0, axis_index_groups=same_core, tiled=True)  23.5 us
    ppermute x4, waiting for transfers between devices, by_chip(): lax.ppermute(back[m], axes, route(m))  10.2 us
    pallas_call x1, Pallas kernels, by_chip(): pl.pallas_call(functools.partial(attend_kernel, core_of, slab_of), out_sh...  6.25 us
    ppermute x4, starting transfers between devices, by_chip(): lax.ppermute(back[m], axes, route(m))  5.11 us
    pallas_call x1, Pallas kernels, by_chip(): pl.pallas_call(functools.partial(prepare_kernel, row_first, head_of), out...  2.15 us
    ppermute x1, waiting for transfers between devices, by_chip(): other = lax.ppermute(mine, axes, [(d, d ^ 1) for d in range(seqs * parts)])  1.81 us
  transfers between devices with their start and end apart: 5, of which 3 were waited for; matrix products, arithmetic and copies ran while one was open for 0% of the time, Pallas kernels for 0%

profile of v3, /device:TPU:0, one launch (start us, length us, event | category | flops | bytes accessed | tf_op | source)
XLA Modules:
  0.0 50.8 jit_solution(15034475852142483281)
XLA Ops:
  0.6 2.2 %prepare.1 = (bf16[16,128,128]{2,1,0:T(8,128)(2,1)}, f32[2,128,128]{2,1,0:T(8,128)}) custom-call(s32[3,128]{1,0:T(4,128)} %pos_hbm.1, f32[64,8]{1,0:T(8,128)} %constant.2.clone.step_hbm, bf16[32,2048]{1,0:T(8,128)(2,1)} %q_hbm.1, bf16[32,2048]{1,0:T(8,128)(2,1)} %k_hbm.1, bf16[32,2048]{1,0:T(8,128)(2,1)} %v_hbm.1, bf16[32,2048]{1,0:T(8,128)(2,1)} %g_hbm.1), custom_call_target="tpu_custom_call" | custom-call | tf_op jit(solution)/shard_map/prepare/pallas_call | solution.py:472
  2.8 0.0 copy-start.2
  2.8 23.5 %all_to_all.5.mine_ref = bf16[16,128,128]{2,1,0:T(8,128)(2,1)S(1)} all-to-all(bf16[16,128,128]{2,1,0:T(8,128)(2,1)} %get-tuple-element.7), channel_id=1, replica_groups={{0,2,4,6,8,10,12,14,16,18,20,22,24,26,28,30},{1,3,5,7,9,11,13,15,17,19,..., dimensions={0} | all-to-all | bytes 1048576 | tf_op jit(solution)/shard_map/all_to_all | solution.py:491
  26.3 0.0 copy-start.1
  26.3 0.0 collective-permute-start
  26.3 0.0 copy-done.2
  26.3 0.1 copy.12.near_ref
  26.4 1.8 %collective-permute-done.other_ref = bf16[16,128,128]{2,1,0:T(8,128)(2,1)S(1)} collective-permute-done((bf16[16,128,128]{2,1,0:T(8,128)(2,1)S(1)}, bf16[16,128,128]{2,1,0:T(8,128)(2,1)S(1)}, u32[]{:S(2)}, u32[]{:S(2)}) %collective-permute-start) | collective-permute-done | bytes 524320 | tf_op jit(solution)/shard_map/ppermute | solution.py:492
  28.2 0.0 copy-done.1
  28.2 6.2 %attend.1 = bf16[4,4,128,128]{3,2,1,0:T(8,128)(2,1)S(1)} custom-call(s32[1024]{0:T(1024)S(1)} %copy-done.1, s32[6,2]{1,0:T(8,128)S(1)} %copy.12.near_ref, bf16[16,128,128]{2,1,0:T(8,128)(2,1)S(1)} %all_to_all.5.mine_ref, bf16[16,128,128]{2,1,0:T(8,128)(2,1)S(1)} %collective-permute-done.other_ref), custom_call_target="tpu_custom_call" | custom-call | tf_op jit(solution)/shard_map/attend/pallas_call | solution.py:493
  34.4 0.0 copy-start
  34.5 1.7 %collective-permute-start.4 = (bf16[4,128,128]{2,1,0:T(8,128)(2,1)S(1)}, bf16[4,128,128]{2,1,0:T(8,128)(2,1)S(1)}, u32[]{:S(2)}, u32[]{:S(2)}) collective-permute-start(bf16[4,128,128]{2,1,0:T(8,128)(2,1)S(1)} %get-tuple-element.8), channel_id=1, source_target_pairs={{0,24},{1,28},{2,26},{3,30},{4,25},{5,29},{6,27},{7,31},{8,16},{9,... | collective-permute-start | bytes 393224 | tf_op jit(solution)/shard_map/ppermute | solution.py:526
  36.2 1.1 %collective-permute-start.3 = (bf16[4,128,128]{2,1,0:T(8,128)(2,1)S(1)}, bf16[4,128,128]{2,1,0:T(8,128)(2,1)S(1)}, u32[]{:S(2)}, u32[]{:S(2)}) collective-permute-start(bf16[4,128,128]{2,1,0:T(8,128)(2,1)S(1)} %get-tuple-element.9), channel_id=1, source_target_pairs={{0,16},{1,20},{2,18},{3,22},{4,17},{5,21},{6,19},{7,23},{8,24},{9,... | collective-permute-start | bytes 393224 | tf_op jit(solution)/shard_map/ppermute | solution.py:526
  37.3 1.7 %collective-permute-start.2 = (bf16[4,128,128]{2,1,0:T(8,128)(2,1)S(1)}, bf16[4,128,128]{2,1,0:T(8,128)(2,1)S(1)}, u32[]{:S(2)}, u32[]{:S(2)}) collective-permute-start(bf16[4,128,128]{2,1,0:T(8,128)(2,1)S(1)} %get-tuple-element.10), channel_id=1, source_target_pairs={{0,8},{1,12},{2,10},{3,14},{4,9},{5,13},{6,11},{7,15},{8,0},{9,4},... | collective-permute-start | bytes 393224 | tf_op jit(solution)/shard_map/ppermute | solution.py:526
  38.9 0.7 %collective-permute-start.1 = (bf16[4,128,128]{2,1,0:T(8,128)(2,1)S(1)}, bf16[4,128,128]{2,1,0:T(8,128)(2,1)S(1)}, u32[]{:S(2)}, u32[]{:S(2)}) collective-permute-start(bf16[4,128,128]{2,1,0:T(8,128)(2,1)S(1)} %get-tuple-element.11), channel_id=1, source_target_pairs={{0,0},{1,4},{2,2},{3,6},{4,1},{5,5},{6,3},{7,7},{8,8},{9,12},{10,1... | collective-permute-start | bytes 393224 | tf_op jit(solution)/shard_map/ppermute | solution.py:526
  39.6 3.2 %collective-permute-done.4.refs_3_ = bf16[4,128,128]{2,1,0:T(8,128)(2,1)S(1)} collective-permute-done((bf16[4,128,128]{2,1,0:T(8,128)(2,1)S(1)}, bf16[4,128,128]{2,1,0:T(8,128)(2,1)S(1)}, u32[]{:S(2)}, u32[]{:S(2)}) %collective-permute-start.4) | collective-permute-done | bytes 131104 | tf_op jit(solution)/shard_map/ppermute | solution.py:526
  42.8 7.0 %collective-permute-done.3.refs_2_ = bf16[4,128,128]{2,1,0:T(8,128)(2,1)S(1)} collective-permute-done((bf16[4,128,128]{2,1,0:T(8,128)(2,1)S(1)}, bf16[4,128,128]{2,1,0:T(8,128)(2,1)S(1)}, u32[]{:S(2)}, u32[]{:S(2)}) %collective-permute-start.3) | collective-permute-done | bytes 131104 | tf_op jit(solution)/shard_map/ppermute | solution.py:526
  49.8 0.0 collective-permute-done.2.refs_1_
  49.8 0.0 collective-permute-done.1.refs_0_
  49.8 0.0 copy-done
  49.9 0.9 %finish.1 = (bf16[128,512]{1,0:T(8,128)(2,1)}, bf16[128,512]{1,0:T(8,128)(2,1)}, bf16[128,512]{1,0:T(8,128)(2,1)}, bf16[128,512]{1,0:T(8,128)(2,1)}) custom-call(f32[2,128,128]{2,1,0:T(8,128)S(1)} %copy-done, bf16[4,128,128]{2,1,0:T(8,128)(2,1)S(1)} %collective-permute-done.1.refs_0_, bf16[4,128,128]{2,1,0:T(8,128)(2,1)S(1)} %collective-permute-done.2.refs_1_, ...), custom_call_target="tpu_custom_call" | custom-call | tf_op jit(solution)/shard_map/finish/pallas_call | solution.py:527
  (1 shorter events, 0.0 us)
Async XLA Ops:
  2.8 23.5 %copy-start.2 = (s32[6,2]{0,1:T(2,128)S(1)}, s32[6,2]{0,1:T(2,128)}, u32[]{:S(2)}) copy-start(s32[6,2]{0,1:T(2,128)} %param.14) | copy-start | bytes 148
  26.3 1.9 %copy-start.1 = (s32[1024]{0:T(1024)S(1)}, s32[1024]{0:T(1024)}, u32[]{:S(2)}) copy-start(s32[1024]{0:T(1024)} %views_ref.1) | copy-start | bytes 12292
  26.3 1.9 %collective-permute-start = (bf16[16,128,128]{2,1,0:T(8,128)(2,1)S(1)}, bf16[16,128,128]{2,1,0:T(8,128)(2,1)S(1)}, u32[]{:S(2)}, u32[]{:S(2)}) collective-permute-start(bf16[16,128,128]{2,1,0:T(8,128)(2,1)S(1)} %all_to_all.5.mine_ref), channel_id=1, source_target_pairs={{0,1},{1,0},{2,3},{3,2},{4,5},{5,4},{6,7},{7,6},{8,9},{9,8},{10,11... | collective-permute-start | bytes 1572872 | tf_op jit(solution)/shard_map/ppermute | solution.py:492
  34.4 15.4 %copy-start = (f32[2,128,128]{2,1,0:T(8,128)S(1)}, f32[2,128,128]{2,1,0:T(8,128)}, u32[]{:S(2)}) copy-start(f32[2,128,128]{2,1,0:T(8,128)} %get-tuple-element.6.table_ref) | copy-start | bytes 393220
  34.5 8.3 %collective-permute-start.4 = (bf16[4,128,128]{2,1,0:T(8,128)(2,1)S(1)}, bf16[4,128,128]{2,1,0:T(8,128)(2,1)S(1)}, u32[]{:S(2)}, u32[]{:S(2)}) collective-permute-start(bf16[4,128,128]{2,1,0:T(8,128)(2,1)S(1)} %get-tuple-element.8), channel_id=1, source_target_pairs={{0,24},{1,28},{2,26},{3,30},{4,25},{5,29},{6,27},{7,31},{8,16},{9,... | collective-permute-start | bytes 393224 | tf_op jit(solution)/shard_map/ppermute | solution.py:526
  36.2 13.7 %collective-permute-start.3 = (bf16[4,128,128]{2,1,0:T(8,128)(2,1)S(1)}, bf16[4,128,128]{2,1,0:T(8,128)(2,1)S(1)}, u32[]{:S(2)}, u32[]{:S(2)}) collective-permute-start(bf16[4,128,128]{2,1,0:T(8,128)(2,1)S(1)} %get-tuple-element.9), channel_id=1, source_target_pairs={{0,16},{1,20},{2,18},{3,22},{4,17},{5,21},{6,19},{7,23},{8,24},{9,... | collective-permute-start | bytes 393224 | tf_op jit(solution)/shard_map/ppermute | solution.py:526
  37.3 12.5 %collective-permute-start.2 = (bf16[4,128,128]{2,1,0:T(8,128)(2,1)S(1)}, bf16[4,128,128]{2,1,0:T(8,128)(2,1)S(1)}, u32[]{:S(2)}, u32[]{:S(2)}) collective-permute-start(bf16[4,128,128]{2,1,0:T(8,128)(2,1)S(1)} %get-tuple-element.10), channel_id=1, source_target_pairs={{0,8},{1,12},{2,10},{3,14},{4,9},{5,13},{6,11},{7,15},{8,0},{9,4},... | collective-permute-start | bytes 393224 | tf_op jit(solution)/shard_map/ppermute | solution.py:526
  38.9 10.9 %collective-permute-start.1 = (bf16[4,128,128]{2,1,0:T(8,128)(2,1)S(1)}, bf16[4,128,128]{2,1,0:T(8,128)(2,1)S(1)}, u32[]{:S(2)}, u32[]{:S(2)}) collective-permute-start(bf16[4,128,128]{2,1,0:T(8,128)(2,1)S(1)} %get-tuple-element.11), channel_id=1, source_target_pairs={{0,0},{1,4},{2,2},{3,6},{4,1},{5,5},{6,3},{7,7},{8,8},{9,12},{10,1... | collective-permute-start | bytes 393224 | tf_op jit(solution)/shard_map/ppermute | solution.py:526

commit v4 on v3

--- a/solution.py
+++ b/solution.py
@@ -232,7 +232,7 @@
 
 LOG2E = math.log2(math.e)
 VMEM_LIMIT = 48 * 1024 * 1024
-PAD = 3
+STANDING = {16: (11, 13, 10, 0, 2, 6, 7, 3, 4, 1, 15, 5, 9, 8, 12, 14)}
 
 
 def whole(space=pltpu.VMEM):
@@ -289,17 +289,20 @@
 
 
 def attend_kernel(
-    core_of, slab_of, views_ref, near_ref, mine_ref, other_ref, out_ref,
-    q_all, g_all, k_all, v_all, kt_all, vt_all, s_all, d_all, p_all, ds_all, dk_all, dv_all, order, rank,
+    core_of, slab_of, standing, views_ref, near_ref, mine_ref, other_ref, out_ref,
+    q_all, g_all, kv_all, kt_all, vt_all, gt_all, s_all, e_all, p_all, ds_all, at_all, dq_all,
+    order, rank, place_of, stand_of,
 ):
     blocks = mine_ref.shape[0] // 2
     rows = mine_ref.shape[1] // 4
     block = 4 * rows
     count = near_ref.shape[0]
     span = count_span(count, blocks)
+    long = blocks - 1 + span
     wide = 2 * block
     core, slab = core_of(), slab_of()
     scale = HD**-0.5
+    factor = scale * LOG2E
     first, held = [], []
     for view in range(count):
         below, equal = 0, 0
@@ -331,108 +334,145 @@
             rank[place + extra] = jnp.int32(i)
         place = place + n
 
-    def spots(pos):
-        at = [pos + PAD]
-        if pos - blocks + PAD >= 0:
-            at.append(pos - blocks + PAD)
-        if pos + blocks < blocks + PAD:
-            at.append(pos + blocks + PAD)
-        return at
-
+    nt = (((1,), (1,)), ((), ()))
+    eye = (
+        lax.broadcasted_iota(jnp.int32, (HD, HD), 0) == lax.broadcasted_iota(jnp.int32, (HD, HD), 1)
+    ).astype(jnp.bfloat16)
+
+    def turn(x):
+        return lax.dot_general(eye, x, nt, preferred_element_type=jnp.float32).astype(jnp.bfloat16)
+
+    for n, chip in enumerate(standing):
+        stand_of[chip] = jnp.int32(n)
     for pos in range(blocks):
         src = order[pos]
-        base = (pos + PAD) * block
+        place_of[src] = jnp.int32(pos)
+        here = slice(pos * block, (pos + 1) * block)
         for at, ref, base in (
-            (0, q_all, pos * block), (1, k_all, base), (2, v_all, base), (3, g_all, pos * block)
+            (0, q_all, pos * block), (1, kv_all, 2 * pos * block), (2, kv_all, (2 * pos + 1) * block), (3, g_all, pos * block)
         ):
             part = slice(at * rows, (at + 1) * rows)
             for x in range(2):
+                n = stand_of[2 * src + x]
                 for whose, c in ((mine_ref, core), (other_ref, 1 - core)):
                     to = pl.ds(pl.multiple_of(base + (2 * x + c) * rows, rows), rows)
-                    ref[to, :] = whose[2 * src + x, part, :]
-        for ref, turned in ((k_all, kt_all), (v_all, vt_all)):
-            source = ref[(pos + PAD) * block : (pos + PAD + 1) * block, :]
-            across = source.astype(jnp.float32).T.astype(jnp.bfloat16)
-            for n, spot in enumerate(spots(pos)):
-                if n:
-                    ref[spot * block : (spot + 1) * block, :] = source
-                turned[:, spot * block : (spot + 1) * block] = across
-    dk_all[...] = jnp.zeros_like(dk_all)
-    dv_all[...] = jnp.zeros_like(dv_all)
-
-    nt = (((1,), (1,)), ((), ()))
-    lane = lax.broadcasted_iota(jnp.int32, (1, wide), 1)
-    second = lane >= block
-
-    for tile in range(blocks // 2):
+                    ref[to, :] = whose[n, part, :]
+        turned = turn(kv_all[2 * pos * block : 2 * (pos + 1) * block, :])
+        for spot in range(pos % blocks, long, blocks):
+            there = slice(spot * block, (spot + 1) * block)
+            kt_all[:, there] = turned[:, :block]
+            vt_all[:HD, there] = turned[:, block:]
+        gt_all[:, here] = turn(g_all[here, :])
+    vt_all[HD:, :] = jnp.ones((vt_all.shape[0] - HD, vt_all.shape[1]), jnp.bfloat16)
+
+    second = lax.broadcasted_iota(jnp.int32, (1, wide), 1) >= block
+    tiles = range(blocks // 2)
+    lanes = [slice(tile * wide, (tile + 1) * wide) for tile in tiles]
+    begins, ats, places, windows, oks = [], [], [], [], []
+    for tile in tiles:
         rank_a, rank_b = rank[2 * tile], rank[2 * tile + 1]
         before = lax.rem(rank_a + count - 1, count)
-        begin = pick(start, rank_a) - pick(size, before) + PAD
-        window = pl.ds(pl.multiple_of(begin * block, block), span * block)
-        q_tile = q_all[tile * wide : (tile + 1) * wide, :]
-        g_tile = g_all[tile * wide : (tile + 1) * wide, :]
-        s_all[...] = lax.dot_general(k_all[window, :], q_tile, nt, preferred_element_type=jnp.float32)
-        d_all[...] = lax.dot_general(v_all[window, :], g_tile, nt, preferred_element_type=jnp.float32)
-        top = jnp.full((1, wide), NEG, jnp.float32)
-        oks = []
-        for i in range(span):
-            at = lax.rem(begin - PAD + i + blocks, blocks)
-            far_a = lax.rem(rank[at] - rank_a + count, count)
-            far_b = lax.rem(rank[at] - rank_b + count, count)
+        begin = lax.rem(pick(start, rank_a) - pick(size, before) + blocks, blocks)
+        begins.append(begin)
+        windows.append(pl.ds(pl.multiple_of(begin * block, block), span * block))
+        at = [lax.rem(begin + i, blocks) for i in range(span)]
+        places.append([pl.multiple_of(n * (2 * block), block) for n in at])
+        oks.append([])
+        for n in at:
+            far_a = lax.rem(rank[n] - rank_a + count, count)
+            far_b = lax.rem(rank[n] - rank_b + count, count)
             ok_a = ((far_a <= 1) | (far_a == count - 1)).astype(jnp.int32)
             ok_b = ((far_b <= 1) | (far_b == count - 1)).astype(jnp.int32)
-            ok = jnp.where(second, ok_b, ok_a) > 0
-            oks.append(ok)
-            part = jnp.where(ok, s_all[i * block : (i + 1) * block, :], NEG)
-            top = jnp.maximum(top, jnp.max(part, axis=0, keepdims=True))
-        factor = scale * LOG2E
-        level = top * factor
-        total = jnp.zeros((1, wide), jnp.float32)
-        delta = jnp.zeros((1, wide), jnp.float32)
+            oks[tile].append(jnp.where(second, ok_b, ok_a) > 0)
+    owned = [place_of[2 * jnp.bitwise_xor(slab, m) + core] for m in range(out_ref.shape[0])]
+    levels, deltas, sums = {}, {}, [0, 0]
+
+    def scores(tile):
+        top = jnp.full((1, wide), NEG, jnp.float32)
+        for i in range(span):
+            s = lax.dot_general(
+                kv_all[pl.ds(places[tile][i], block), :], q_all[lanes[tile], :], nt, preferred_element_type=jnp.float32
+            )
+            s_all[tile, i] = s
+            top = jnp.maximum(top, jnp.where(oks[tile][i], jnp.max(s, axis=0, keepdims=True), NEG))
+        levels[tile] = top * factor
+
+    def weights(tile):
+        for i in range(span):
+            e = jnp.exp2(s_all[tile, i] * factor - jnp.where(oks[tile][i], levels[tile], -NEG))
+            e_all[tile, i * block : (i + 1) * block, :] = e.astype(jnp.bfloat16)
+
+    def outputs(tile):
+        out = jnp.dot(vt_all[:, windows[tile]], e_all[tile], preferred_element_type=jnp.float32)
+        total = out[HD : HD + 1, :]
+        out = out[:HD, :] / total
+        at_all[:, lanes[tile]] = out.astype(jnp.bfloat16)
+        deltas[tile] = jnp.sum(gt_all[:, lanes[tile]].astype(jnp.float32) * out, axis=0, keepdims=True)
+        levels[tile] = levels[tile] + jnp.log2(total)
+
+    def slopes(tile):
         for i in range(span):
             here = slice(i * block, (i + 1) * block)
-            e = jnp.where(oks[i], jnp.exp2(s_all[here, :] * factor - level), 0.0)
-            s_all[here, :] = e
-            total = total + jnp.sum(e, axis=0, keepdims=True)
-            delta = delta + jnp.sum(e * d_all[here, :], axis=0, keepdims=True)
-            ds_all[here, :] = e.astype(jnp.bfloat16)
-        share = 1.0 / total
-        delta = delta * share
-        out_t = jnp.dot(vt_all[:, window], ds_all[...], preferred_element_type=jnp.float32) * share
-        for i in range(span):
-            here = slice(i * block, (i + 1) * block)
-            p = s_all[here, :] * share
-            p_all[here, :] = p.astype(jnp.bfloat16)
-            ds_all[here, :] = (p * (d_all[here, :] - delta)).astype(jnp.bfloat16)
-        dq_t = jnp.dot(kt_all[:, window], ds_all[...], preferred_element_type=jnp.float32) * scale
-        dv_all[window, :] += jnp.dot(p_all[...], g_tile, preferred_element_type=jnp.float32)
-        dk_all[window, :] += jnp.dot(ds_all[...], q_tile, preferred_element_type=jnp.float32)
-        for at in range(2):
-            src = order[2 * tile + at]
-
-            @pl.when(lax.rem(src, 2) == core)
-            def _():
-                to = jnp.bitwise_xor(src // 2, slab)
-                out_ref[to, 0] = out_t[:, at * block : (at + 1) * block].T.astype(jnp.bfloat16)
-                out_ref[to, 1] = dq_t[:, at * block : (at + 1) * block].T.astype(jnp.bfloat16)
-
-    for pos in range(blocks):
-        src = order[pos]
-
-        @pl.when(lax.rem(src, 2) == core)
-        def _():
-            to = jnp.bitwise_xor(src // 2, slab)
-            dk = sum(dk_all[spot * block : (spot + 1) * block, :] for spot in spots(pos))
-            dv = sum(dv_all[spot * block : (spot + 1) * block, :] for spot in spots(pos))
-            out_ref[to, 2] = (dk * scale).astype(jnp.bfloat16)
-            out_ref[to, 3] = dv.astype(jnp.bfloat16)
-
-
-def finish_kernel(slab_of, table_ref, *refs):
+            d = lax.dot_general(
+                kv_all[pl.ds(places[tile][i] + block, block), :], g_all[lanes[tile], :], nt, preferred_element_type=jnp.float32
+            )
+            p = jnp.exp2(s_all[tile, i] * factor - jnp.where(oks[tile][i], levels[tile], -NEG))
+            p_all[tile, here, :] = p.astype(jnp.bfloat16)
+            ds_all[tile, here, :] = (p * (d - deltas[tile])).astype(jnp.bfloat16)
+        p_all[tile, span * block :, :] = jnp.zeros((block, wide), jnp.bfloat16)
+        ds_all[tile, span * block :, :] = jnp.zeros((block, wide), jnp.bfloat16)
+
+    def query_slopes(tile):
+        dq = jnp.dot(kt_all[:, windows[tile]], ds_all[tile, : span * block, :], preferred_element_type=jnp.float32)
+        dq_all[:, lanes[tile]] = (dq * scale).astype(jnp.bfloat16)
+
+    def key_slopes(tile):
+        rels = [
+            pl.multiple_of(jnp.minimum(lax.rem(pos - begins[tile] + blocks, blocks), span) * block, block)
+            for pos in owned
+        ]
+        for n, (ref, other) in enumerate(((ds_all, q_all), (p_all, g_all))):
+            x = jnp.concatenate([ref[tile, pl.ds(rel, block), :] for rel in rels], axis=0)
+            sums[n] = sums[n] + jnp.dot(x, other[lanes[tile], :], preferred_element_type=jnp.float32)
+
+    scores(0)
+    weights(0)
+    scores(1)
+    weights(1)
+    scores(2)
+    weights(2)
+    scores(3)
+    weights(3)
+    outputs(0)
+    outputs(1)
+    outputs(2)
+    outputs(3)
+    slopes(0)
+    slopes(1)
+    slopes(2)
+    slopes(3)
+    query_slopes(0)
+    query_slopes(1)
+    query_slopes(2)
+    query_slopes(3)
+    key_slopes(0)
+    key_slopes(1)
+    key_slopes(2)
+    key_slopes(3)
+    dk, dv = sums
+    for m, pos in enumerate(owned):
+        here = pl.ds(pl.multiple_of(pos * block, block), block)
+        out_ref[m, 0] = turn(at_all[:, here])
+        out_ref[m, 1] = turn(dq_all[:, here])
+        out_ref[m, 2] = (dk[m * block : (m + 1) * block] * scale).astype(jnp.bfloat16)
+        out_ref[m, 3] = dv[m * block : (m + 1) * block].astype(jnp.bfloat16)
+
+
+def finish_kernel(slab_of, turns, table_ref, *refs):
     chunks, outs = refs[:-4], refs[-4:]
     slab = slab_of()
     cosine, sine = table_ref[0], table_ref[1]
-    for m, ref in enumerate(chunks):
+    for m, ref in zip(turns, chunks, strict=True):
         lanes = pl.ds(pl.multiple_of(jnp.bitwise_xor(slab, m) * HD, HD), HD)
         for at, out in enumerate(outs):
             x = ref[at]
@@ -454,9 +494,10 @@
     chips = seqs * xs
     block = rows * parts
     span = count_span(adjacency.shape[0], seqs)
-    long = seqs + 2 * PAD
+    tokens = seqs * block
     wide = 2 * block
-    head_of = [((c % xs) * 2 + (c // xs) % 2) * group + c // xs // 2 for c in range(chips)]
+    standing = STANDING.get(chips, tuple(range(chips)))
+    head_of = [((c % xs) * 2 + (c // xs) % 2) * group + c // xs // 2 for c in standing]
     limits = pltpu.CompilerParams(vmem_limit_bytes=VMEM_LIMIT)
 
     def row_first():
@@ -483,33 +524,33 @@
             *[pltpu.VMEM((rows, width), jnp.bfloat16)] * 4,
             pltpu.SemaphoreType.DMA((6,)),
         ],
-        compiler_params=pltpu.CompilerParams(vmem_limit_bytes=60*1024*1024),
+        compiler_params=pltpu.CompilerParams(vmem_limit_bytes=VMEM_LIMIT + 12 * 1024 * 1024),
         name="prepare",
     )(positions, jnp.asarray(steps), q_in, k_in, v_in, grad_out)
     axes = ("seq", "head")
-    same_core = [[(c // xs) * parts + (c % xs) * 2 + core for c in range(chips)] for core in range(2)]
+    same_core = [[(c // xs) * parts + (c % xs) * 2 + core for c in standing] for core in range(2)]
     mine = lax.all_to_all(sent, axes, 0, 0, axis_index_groups=same_core, tiled=True)
     other = lax.ppermute(mine, axes, [(d, d ^ 1) for d in range(seqs * parts)])
     back = pl.pallas_call(
-        functools.partial(attend_kernel, core_of, slab_of),
+        functools.partial(attend_kernel, core_of, slab_of, standing),
         out_shape=jax.ShapeDtypeStruct((group, 4, block, HD), jnp.bfloat16),
         in_specs=[whole(pltpu.SMEM), whole(pltpu.SMEM), whole(), whole()],
         out_specs=whole(),
         scratch_shapes=[
-            pltpu.VMEM((seqs * block, HD), jnp.bfloat16),
-            pltpu.VMEM((seqs * block, HD), jnp.bfloat16),
-            pltpu.VMEM((long * block, HD), jnp.bfloat16),
-            pltpu.VMEM((long * block, HD), jnp.bfloat16),
-            pltpu.VMEM((HD, long * block), jnp.bfloat16),
-            pltpu.VMEM((HD, long * block), jnp.bfloat16),
-            pltpu.VMEM((span * block, wide), jnp.float32),
-            pltpu.VMEM((span * block, wide), jnp.float32),
-            pltpu.VMEM((span * block, wide), jnp.bfloat16),
-            pltpu.VMEM((span * block, wide), jnp.bfloat16),
-            pltpu.VMEM((long * block, HD), jnp.float32),
-            pltpu.VMEM((long * block, HD), jnp.float32),
-            pltpu.SMEM((seqs + 1,), jnp.int32),
-            pltpu.SMEM((seqs + 1,), jnp.int32),
+            pltpu.VMEM((tokens, HD), jnp.bfloat16),
+            pltpu.VMEM((tokens, HD), jnp.bfloat16),
+            pltpu.VMEM((2 * tokens, HD), jnp.bfloat16),
+            pltpu.VMEM((HD, tokens + (span - 1) * block), jnp.bfloat16),
+            pltpu.VMEM((HD + 16, tokens + (span - 1) * block), jnp.bfloat16),
+            pltpu.VMEM((HD, tokens), jnp.bfloat16),
+            pltpu.VMEM((seqs // 2, span, block, wide), jnp.float32),
+            pltpu.VMEM((seqs // 2, span * block, wide), jnp.bfloat16),
+            pltpu.VMEM((seqs // 2, (span + 1) * block, wide), jnp.bfloat16),
+            pltpu.VMEM((seqs // 2, (span + 1) * block, wide), jnp.bfloat16),
+            pltpu.VMEM((HD, tokens), jnp.bfloat16),
+            pltpu.VMEM((HD, tokens), jnp.bfloat16),
+            *[pltpu.SMEM((seqs + 1,), jnp.int32)] * 3,
+            pltpu.SMEM((chips,), jnp.int32),
         ],
         compiler_params=limits,
         name="attend",
@@ -523,15 +564,16 @@
             pairs.append((d, to_s * parts + h // 2 * 2 + s % 2))
         return pairs
 
-    chunks = {m: lax.ppermute(back[m], axes, route(m)) for m in reversed(range(group))}
+    turns = [(group // 2 - n) % group for n in reversed(range(group))]
+    chunks = [lax.ppermute(back[m], axes, route(m)) for m in turns]
     return pl.pallas_call(
-        functools.partial(finish_kernel, slab_of),
+        functools.partial(finish_kernel, slab_of, turns),
         out_shape=(jax.ShapeDtypeStruct((block, group * HD), jnp.bfloat16),) * 4,
         in_specs=[whole()] * (1 + group),
         out_specs=(whole(),) * 4,
         compiler_params=limits,
         name="finish",
-    )(table, *[chunks[m] for m in range(group)])
+    )(table, *chunks)
 
 
 def solution(mesh):

time: 51 us -> 44.8 us (0.88)
  blocking collectives: 23.5 us -> 19.9 us
  Pallas kernels: 9.31 us -> 6.99 us
  waiting for transfers between devices: 12 us -> 10.8 us
  starting transfers between devices: 5.11 us -> 5.63 us
    all_to_all x1, blocking collectives: 23.5 us -> 19.9 us  [by_chip(): lax.all_to_all(sent, axes, 0, 0, axis_index_groups=same_core, tiled=True)]
    pallas_call x2, Pallas kernels: 7.16 us -> 4.84 us  [the longest x1 3.93 us: by_chip(): pl.pallas_call(functools.partial(attend_kernel, core_of, slab_of, standin...]
    ppermute x4, waiting for transfers between devices: 10.2 us -> 8.95 us  [by_chip(): chunks = [lax.ppermute(back[m], axes, route(m)) for m in turns]]
    ppermute x4, starting transfers between devices: 5.11 us -> 5.63 us  [by_chip(): chunks = [lax.ppermute(back[m], axes, route(m)) for m in turns]]
where the time goes in v4:
time: 44.8 us; the launch traced here: 44.1 us
  blocking collectives  19.9 us (44%)
  waiting for transfers between devices  10.8 us (24%)
  Pallas kernels  6.99 us (16%)
  starting transfers between devices  5.63 us (13%)
  between operations  0.69 us (2%)
    all_to_all x1, blocking collectives, by_chip(): lax.all_to_all(sent, axes, 0, 0, axis_index_groups=same_core, tiled=True)  19.9 us
    ppermute x4, waiting for transfers between devices, by_chip(): chunks = [lax.ppermute(back[m], axes, route(m)) for m in turns]  8.95 us
    ppermute x4, starting transfers between devices, by_chip(): chunks = [lax.ppermute(back[m], axes, route(m)) for m in turns]  5.63 us
    pallas_call x1, Pallas kernels, by_chip(): pl.pallas_call(functools.partial(attend_kernel, core_of, slab_of, standin...  3.93 us
    pallas_call x1, Pallas kernels, by_chip(): pl.pallas_call(functools.partial(prepare_kernel, row_first, head_of), out...  2.15 us
    ppermute x1, waiting for transfers between devices, by_chip(): other = lax.ppermute(mine, axes, [(d, d ^ 1) for d in range(seqs * parts)])  1.81 us
    pallas_call x1, Pallas kernels, by_chip(): pl.pallas_call(functools.partial(finish_kernel, slab_of, turns), out_shap...  0.91 us
  transfers between devices with their start and end apart: 5, of which 3 were waited for; matrix products, arithmetic and copies ran while one was open for 0% of the time, Pallas kernels for 0%

profile of v4, /device:TPU:0, one launch (start us, length us, event | category | flops | bytes accessed | tf_op | source)
XLA Modules:
  0.0 44.1 jit_solution(1247832879558369037)
XLA Ops:
  0.6 2.2 %prepare.1 = (bf16[16,128,128]{2,1,0:T(8,128)(2,1)}, f32[2,128,128]{2,1,0:T(8,128)}) custom-call(s32[3,128]{1,0:T(4,128)} %pos_hbm.1, f32[64,8]{1,0:T(8,128)} %constant.2.clone.step_hbm, bf16[32,2048]{1,0:T(8,128)(2,1)} %q_hbm.1, bf16[32,2048]{1,0:T(8,128)(2,1)} %k_hbm.1, bf16[32,2048]{1,0:T(8,128)(2,1)} %v_hbm.1, bf16[32,2048]{1,0:T(8,128)(2,1)} %g_hbm.1), custom_call_target="tpu_custom_call" | custom-call | tf_op jit(solution)/shard_map/prepare/pallas_call | solution.py:513
  2.8 0.0 copy-start.2
  2.8 19.9 %all_to_all.5.mine_ref = bf16[16,128,128]{2,1,0:T(8,128)(2,1)S(1)} all-to-all(bf16[16,128,128]{2,1,0:T(8,128)(2,1)} %get-tuple-element.7), channel_id=1, replica_groups={{22,26,20,0,4,12,14,6,8,2,30,10,18,16,24,28},{23,27,21,1,5,13,15,7,9,3,..., dimensions={0} | all-to-all | bytes 1048576 | tf_op jit(solution)/shard_map/all_to_all | solution.py:532
  22.7 0.0 copy-start.1
  22.7 0.0 collective-permute-start
  22.7 0.0 copy-done.2
  22.7 0.1 copy.12.near_ref
  22.8 1.8 %collective-permute-done.other_ref = bf16[16,128,128]{2,1,0:T(8,128)(2,1)S(1)} collective-permute-done((bf16[16,128,128]{2,1,0:T(8,128)(2,1)S(1)}, bf16[16,128,128]{2,1,0:T(8,128)(2,1)S(1)}, u32[]{:S(2)}, u32[]{:S(2)}) %collective-permute-start) | collective-permute-done | bytes 524320 | tf_op jit(solution)/shard_map/ppermute | solution.py:533
  24.6 0.0 copy-done.1
  24.6 3.9 %attend.1 = bf16[4,4,128,128]{3,2,1,0:T(8,128)(2,1)S(1)} custom-call(s32[1024]{0:T(1024)S(1)} %copy-done.1, s32[6,2]{1,0:T(8,128)S(1)} %copy.12.near_ref, bf16[16,128,128]{2,1,0:T(8,128)(2,1)S(1)} %all_to_all.5.mine_ref, bf16[16,128,128]{2,1,0:T(8,128)(2,1)S(1)} %collective-permute-done.other_ref), custom_call_target="tpu_custom_call" | custom-call | tf_op jit(solution)/shard_map/attend/pallas_call | solution.py:534
  28.6 0.0 copy-start
  28.6 3.4 %collective-permute-start.4 = (bf16[4,128,128]{2,1,0:T(8,128)(2,1)S(1)}, bf16[4,128,128]{2,1,0:T(8,128)(2,1)S(1)}, u32[]{:S(2)}, u32[]{:S(2)}) collective-permute-start(bf16[4,128,128]{2,1,0:T(8,128)(2,1)S(1)} %get-tuple-element.8), channel_id=1, source_target_pairs={{0,16},{1,20},{2,18},{3,22},{4,17},{5,21},{6,19},{7,23},{8,24},{9,... | collective-permute-start | bytes 393224 | tf_op jit(solution)/shard_map/ppermute | solution.py:568
  32.0 0.7 %collective-permute-start.3 = (bf16[4,128,128]{2,1,0:T(8,128)(2,1)S(1)}, bf16[4,128,128]{2,1,0:T(8,128)(2,1)S(1)}, u32[]{:S(2)}, u32[]{:S(2)}) collective-permute-start(bf16[4,128,128]{2,1,0:T(8,128)(2,1)S(1)} %get-tuple-element.9), channel_id=1, source_target_pairs={{0,8},{1,12},{2,10},{3,14},{4,9},{5,13},{6,11},{7,15},{8,0},{9,4},... | collective-permute-start | bytes 393224 | tf_op jit(solution)/shard_map/ppermute | solution.py:568
  32.7 0.7 %collective-permute-start.2 = (bf16[4,128,128]{2,1,0:T(8,128)(2,1)S(1)}, bf16[4,128,128]{2,1,0:T(8,128)(2,1)S(1)}, u32[]{:S(2)}, u32[]{:S(2)}) collective-permute-start(bf16[4,128,128]{2,1,0:T(8,128)(2,1)S(1)} %get-tuple-element.10), channel_id=1, source_target_pairs={{0,0},{1,4},{2,2},{3,6},{4,1},{5,5},{6,3},{7,7},{8,8},{9,12},{10,1... | collective-permute-start | bytes 393224 | tf_op jit(solution)/shard_map/ppermute | solution.py:568
  33.4 0.9 %collective-permute-start.1 = (bf16[4,128,128]{2,1,0:T(8,128)(2,1)S(1)}, bf16[4,128,128]{2,1,0:T(8,128)(2,1)S(1)}, u32[]{:S(2)}, u32[]{:S(2)}) collective-permute-start(bf16[4,128,128]{2,1,0:T(8,128)(2,1)S(1)} %get-tuple-element.11), channel_id=1, source_target_pairs={{0,24},{1,28},{2,26},{3,30},{4,25},{5,29},{6,27},{7,31},{8,16},{9,... | collective-permute-start | bytes 393224 | tf_op jit(solution)/shard_map/ppermute | solution.py:568
  34.3 4.3 %collective-permute-done.4.refs_3_ = bf16[4,128,128]{2,1,0:T(8,128)(2,1)S(1)} collective-permute-done((bf16[4,128,128]{2,1,0:T(8,128)(2,1)S(1)}, bf16[4,128,128]{2,1,0:T(8,128)(2,1)S(1)}, u32[]{:S(2)}, u32[]{:S(2)}) %collective-permute-start.4) | collective-permute-done | bytes 131104 | tf_op jit(solution)/shard_map/ppermute | solution.py:568
  38.5 4.7 %collective-permute-done.3.refs_2_ = bf16[4,128,128]{2,1,0:T(8,128)(2,1)S(1)} collective-permute-done((bf16[4,128,128]{2,1,0:T(8,128)(2,1)S(1)}, bf16[4,128,128]{2,1,0:T(8,128)(2,1)S(1)}, u32[]{:S(2)}, u32[]{:S(2)}) %collective-permute-start.3) | collective-permute-done | bytes 131104 | tf_op jit(solution)/shard_map/ppermute | solution.py:568
  43.2 0.0 collective-permute-done.2.refs_1_
  43.2 0.0 collective-permute-done.1.refs_0_
  43.2 0.0 copy-done
  43.2 0.9 %finish.1 = (bf16[128,512]{1,0:T(8,128)(2,1)}, bf16[128,512]{1,0:T(8,128)(2,1)}, bf16[128,512]{1,0:T(8,128)(2,1)}, bf16[128,512]{1,0:T(8,128)(2,1)}) custom-call(f32[2,128,128]{2,1,0:T(8,128)S(1)} %copy-done, bf16[4,128,128]{2,1,0:T(8,128)(2,1)S(1)} %collective-permute-done.1.refs_0_, bf16[4,128,128]{2,1,0:T(8,128)(2,1)S(1)} %collective-permute-done.2.refs_1_, ...), custom_call_target="tpu_custom_call" | custom-call | tf_op jit(solution)/shard_map/finish/pallas_call | solution.py:569
  (1 shorter events, 0.0 us)
Async XLA Ops:
  2.8 19.9 %copy-start.2 = (s32[6,2]{0,1:T(2,128)S(1)}, s32[6,2]{0,1:T(2,128)}, u32[]{:S(2)}) copy-start(s32[6,2]{0,1:T(2,128)} %param.14) | copy-start | bytes 148
  22.7 1.9 %copy-start.1 = (s32[1024]{0:T(1024)S(1)}, s32[1024]{0:T(1024)}, u32[]{:S(2)}) copy-start(s32[1024]{0:T(1024)} %views_ref.1) | copy-start | bytes 12292
  22.7 1.9 %collective-permute-start = (bf16[16,128,128]{2,1,0:T(8,128)(2,1)S(1)}, bf16[16,128,128]{2,1,0:T(8,128)(2,1)S(1)}, u32[]{:S(2)}, u32[]{:S(2)}) collective-permute-start(bf16[16,128,128]{2,1,0:T(8,128)(2,1)S(1)} %all_to_all.5.mine_ref), channel_id=1, source_target_pairs={{0,1},{1,0},{2,3},{3,2},{4,5},{5,4},{6,7},{7,6},{8,9},{9,8},{10,11... | collective-permute-start | bytes 1572872 | tf_op jit(solution)/shard_map/ppermute | solution.py:533
  28.6 14.6 %copy-start = (f32[2,128,128]{2,1,0:T(8,128)S(1)}, f32[2,128,128]{2,1,0:T(8,128)}, u32[]{:S(2)}) copy-start(f32[2,128,128]{2,1,0:T(8,128)} %get-tuple-element.6.table_ref) | copy-start | bytes 393220
  28.6 9.9 %collective-permute-start.4 = (bf16[4,128,128]{2,1,0:T(8,128)(2,1)S(1)}, bf16[4,128,128]{2,1,0:T(8,128)(2,1)S(1)}, u32[]{:S(2)}, u32[]{:S(2)}) collective-permute-start(bf16[4,128,128]{2,1,0:T(8,128)(2,1)S(1)} %get-tuple-element.8), channel_id=1, source_target_pairs={{0,16},{1,20},{2,18},{3,22},{4,17},{5,21},{6,19},{7,23},{8,24},{9,... | collective-permute-start | bytes 393224 | tf_op jit(solution)/shard_map/ppermute | solution.py:568
  32.0 11.2 %collective-permute-start.3 = (bf16[4,128,128]{2,1,0:T(8,128)(2,1)S(1)}, bf16[4,128,128]{2,1,0:T(8,128)(2,1)S(1)}, u32[]{:S(2)}, u32[]{:S(2)}) collective-permute-start(bf16[4,128,128]{2,1,0:T(8,128)(2,1)S(1)} %get-tuple-element.9), channel_id=1, source_target_pairs={{0,8},{1,12},{2,10},{3,14},{4,9},{5,13},{6,11},{7,15},{8,0},{9,4},... | collective-permute-start | bytes 393224 | tf_op jit(solution)/shard_map/ppermute | solution.py:568
  32.7 10.5 %collective-permute-start.2 = (bf16[4,128,128]{2,1,0:T(8,128)(2,1)S(1)}, bf16[4,128,128]{2,1,0:T(8,128)(2,1)S(1)}, u32[]{:S(2)}, u32[]{:S(2)}) collective-permute-start(bf16[4,128,128]{2,1,0:T(8,128)(2,1)S(1)} %get-tuple-element.10), channel_id=1, source_target_pairs={{0,0},{1,4},{2,2},{3,6},{4,1},{5,5},{6,3},{7,7},{8,8},{9,12},{10,1... | collective-permute-start | bytes 393224 | tf_op jit(solution)/shard_map/ppermute | solution.py:568
  33.4 9.8 %collective-permute-start.1 = (bf16[4,128,128]{2,1,0:T(8,128)(2,1)S(1)}, bf16[4,128,128]{2,1,0:T(8,128)(2,1)S(1)}, u32[]{:S(2)}, u32[]{:S(2)}) collective-permute-start(bf16[4,128,128]{2,1,0:T(8,128)(2,1)S(1)} %get-tuple-element.11), channel_id=1, source_target_pairs={{0,24},{1,28},{2,26},{3,30},{4,25},{5,29},{6,27},{7,31},{8,16},{9,... | collective-permute-start | bytes 393224 | tf_op jit(solution)/shard_map/ppermute | solution.py:568

commit v5 on v4

--- a/solution.py
+++ b/solution.py
@@ -510,6 +510,7 @@
         return lax.axis_index("seq") // 2
 
     steps = inverse_steps()
+    loaded = (positions, jnp.asarray(steps), q_in, k_in, v_in, grad_out)
     sent, table = pl.pallas_call(
         functools.partial(prepare_kernel, row_first, head_of),
         out_shape=(
@@ -524,9 +525,9 @@
             *[pltpu.VMEM((rows, width), jnp.bfloat16)] * 4,
             pltpu.SemaphoreType.DMA((6,)),
         ],
-        compiler_params=pltpu.CompilerParams(vmem_limit_bytes=VMEM_LIMIT + 12 * 1024 * 1024),
+        compiler_params=limits,
         name="prepare",
-    )(positions, jnp.asarray(steps), q_in, k_in, v_in, grad_out)
+    )(*[pltpu.with_memory_space_constraint(x, pltpu.HBM) for x in loaded])
     axes = ("seq", "head")
     same_core = [[(c // xs) * parts + (c % xs) * 2 + core for c in standing] for core in range(2)]
     mine = lax.all_to_all(sent, axes, 0, 0, axis_index_groups=same_core, tiled=True)

time: 44.8 us -> 43.1 us (0.962)
  blocking collectives: 19.9 us -> 19 us
  Pallas kernels: 6.99 us -> 6.22 us
    all_to_all x1, blocking collectives: 19.9 us -> 19 us  [by_chip(): lax.all_to_all(sent, axes, 0, 0, axis_index_groups=same_core, tiled=True)]
    pallas_call x1, Pallas kernels: 2.15 us -> 1.37 us  [by_chip(): pl.pallas_call(functools.partial(prepare_kernel, row_first, head_of), out...]
where the time goes in v5:
time: 43.1 us; the launch traced here: 42.4 us
  blocking collectives  19 us (44%)
  waiting for transfers between devices  10.7 us (25%)
  Pallas kernels  6.22 us (14%)
  starting transfers between devices  5.59 us (13%)
  between operations  0.68 us (2%)
    all_to_all x1, blocking collectives, by_chip(): lax.all_to_all(sent, axes, 0, 0, axis_index_groups=same_core, tiled=True)  19 us
    ppermute x4, waiting for transfers between devices, by_chip(): chunks = [lax.ppermute(back[m], axes, route(m)) for m in turns]  8.93 us
    ppermute x4, starting transfers between devices, by_chip(): chunks = [lax.ppermute(back[m], axes, route(m)) for m in turns]  5.58 us
    pallas_call x1, Pallas kernels, by_chip(): pl.pallas_call(functools.partial(attend_kernel, core_of, slab_of, standin...  3.93 us
    ppermute x1, waiting for transfers between devices, by_chip(): other = lax.ppermute(mine, axes, [(d, d ^ 1) for d in range(seqs * parts)])  1.81 us
    pallas_call x1, Pallas kernels, by_chip(): pl.pallas_call(functools.partial(prepare_kernel, row_first, head_of), out...  1.37 us
    pallas_call x1, Pallas kernels, by_chip(): pl.pallas_call(functools.partial(finish_kernel, slab_of, turns), out_shap...  0.91 us
  transfers between devices with their start and end apart: 5, of which 3 were waited for; matrix products, arithmetic and copies ran while one was open for 0% of the time, Pallas kernels for 0%

profile of v5, /device:TPU:0, one launch (start us, length us, event | category | flops | bytes accessed | tf_op | source)
XLA Modules:
  0.0 42.4 jit_solution(4727338323586990394)
XLA Ops:
  0.6 1.4 %prepare.1 = (bf16[16,128,128]{2,1,0:T(8,128)(2,1)S(1)}, f32[2,128,128]{2,1,0:T(8,128)S(1)}) custom-call(s32[3,128]{1,0:T(4,128)} %pos_hbm.1, f32[64,8]{1,0:T(8,128)} %constant.2.clone.step_hbm, bf16[32,2048]{1,0:T(8,128)(2,1)} %q_hbm.1, bf16[32,2048]{1,0:T(8,128)(2,1)} %k_hbm.1, bf16[32,2048]{1,0:T(8,128)(2,1)} %v_hbm.1, bf16[32,2048]{1,0:T(8,128)(2,1)} %g_hbm.1), custom_call_target="tpu_custom_call" | custom-call | tf_op jit(solution)/shard_map/prepare/pallas_call | solution.py:514
  2.0 0.0 copy-start.1
  2.0 19.0 %all_to_all.5.mine_ref = bf16[16,128,128]{2,1,0:T(8,128)(2,1)S(1)} all-to-all(bf16[16,128,128]{2,1,0:T(8,128)(2,1)S(1)} %get-tuple-element.7), channel_id=1, replica_groups={{22,26,20,0,4,12,14,6,8,2,30,10,18,16,24,28},{23,27,21,1,5,13,15,7,9,3,..., dimensions={0} | all-to-all | bytes 1048576 | tf_op jit(solution)/shard_map/all_to_all | solution.py:533
  21.1 0.0 copy-start
  21.1 0.0 collective-permute-start
  21.1 0.0 copy-done.1
  21.1 0.1 copy.12.near_ref
  21.2 1.8 %collective-permute-done.other_ref = bf16[16,128,128]{2,1,0:T(8,128)(2,1)S(1)} collective-permute-done((bf16[16,128,128]{2,1,0:T(8,128)(2,1)S(1)}, bf16[16,128,128]{2,1,0:T(8,128)(2,1)S(1)}, u32[]{:S(2)}, u32[]{:S(2)}) %collective-permute-start) | collective-permute-done | bytes 524320 | tf_op jit(solution)/shard_map/ppermute | solution.py:534
  23.0 0.0 copy-done
  23.0 3.9 %attend.1 = bf16[4,4,128,128]{3,2,1,0:T(8,128)(2,1)S(1)} custom-call(s32[1024]{0:T(1024)S(1)} %copy-done, s32[6,2]{1,0:T(8,128)S(1)} %copy.12.near_ref, bf16[16,128,128]{2,1,0:T(8,128)(2,1)S(1)} %all_to_all.5.mine_ref, bf16[16,128,128]{2,1,0:T(8,128)(2,1)S(1)} %collective-permute-done.other_ref), custom_call_target="tpu_custom_call" | custom-call | tf_op jit(solution)/shard_map/attend/pallas_call | solution.py:535
  27.0 3.3 %collective-permute-start.4 = (bf16[4,128,128]{2,1,0:T(8,128)(2,1)S(1)}, bf16[4,128,128]{2,1,0:T(8,128)(2,1)S(1)}, u32[]{:S(2)}, u32[]{:S(2)}) collective-permute-start(bf16[4,128,128]{2,1,0:T(8,128)(2,1)S(1)} %get-tuple-element.8), channel_id=1, source_target_pairs={{0,16},{1,20},{2,18},{3,22},{4,17},{5,21},{6,19},{7,23},{8,24},{9,... | collective-permute-start | bytes 393224 | tf_op jit(solution)/shard_map/ppermute | solution.py:569
  30.3 0.8 %collective-permute-start.3 = (bf16[4,128,128]{2,1,0:T(8,128)(2,1)S(1)}, bf16[4,128,128]{2,1,0:T(8,128)(2,1)S(1)}, u32[]{:S(2)}, u32[]{:S(2)}) collective-permute-start(bf16[4,128,128]{2,1,0:T(8,128)(2,1)S(1)} %get-tuple-element.9), channel_id=1, source_target_pairs={{0,8},{1,12},{2,10},{3,14},{4,9},{5,13},{6,11},{7,15},{8,0},{9,4},... | collective-permute-start | bytes 393224 | tf_op jit(solution)/shard_map/ppermute | solution.py:569
  31.1 0.7 %collective-permute-start.2 = (bf16[4,128,128]{2,1,0:T(8,128)(2,1)S(1)}, bf16[4,128,128]{2,1,0:T(8,128)(2,1)S(1)}, u32[]{:S(2)}, u32[]{:S(2)}) collective-permute-start(bf16[4,128,128]{2,1,0:T(8,128)(2,1)S(1)} %get-tuple-element.10), channel_id=1, source_target_pairs={{0,0},{1,4},{2,2},{3,6},{4,1},{5,5},{6,3},{7,7},{8,8},{9,12},{10,1... | collective-permute-start | bytes 393224 | tf_op jit(solution)/shard_map/ppermute | solution.py:569
  31.7 0.8 %collective-permute-start.1 = (bf16[4,128,128]{2,1,0:T(8,128)(2,1)S(1)}, bf16[4,128,128]{2,1,0:T(8,128)(2,1)S(1)}, u32[]{:S(2)}, u32[]{:S(2)}) collective-permute-start(bf16[4,128,128]{2,1,0:T(8,128)(2,1)S(1)} %get-tuple-element.11), channel_id=1, source_target_pairs={{0,24},{1,28},{2,26},{3,30},{4,25},{5,29},{6,27},{7,31},{8,16},{9,... | collective-permute-start | bytes 393224 | tf_op jit(solution)/shard_map/ppermute | solution.py:569
  32.6 4.2 %collective-permute-done.4.refs_3_ = bf16[4,128,128]{2,1,0:T(8,128)(2,1)S(1)} collective-permute-done((bf16[4,128,128]{2,1,0:T(8,128)(2,1)S(1)}, bf16[4,128,128]{2,1,0:T(8,128)(2,1)S(1)}, u32[]{:S(2)}, u32[]{:S(2)}) %collective-permute-start.4) | collective-permute-done | bytes 131104 | tf_op jit(solution)/shard_map/ppermute | solution.py:569
  36.8 4.7 %collective-permute-done.3.refs_2_ = bf16[4,128,128]{2,1,0:T(8,128)(2,1)S(1)} collective-permute-done((bf16[4,128,128]{2,1,0:T(8,128)(2,1)S(1)}, bf16[4,128,128]{2,1,0:T(8,128)(2,1)S(1)}, u32[]{:S(2)}, u32[]{:S(2)}) %collective-permute-start.3) | collective-permute-done | bytes 131104 | tf_op jit(solution)/shard_map/ppermute | solution.py:569
  41.5 0.0 collective-permute-done.2.refs_1_
  41.5 0.0 collective-permute-done.1.refs_0_
  41.5 0.9 %finish.1 = (bf16[128,512]{1,0:T(8,128)(2,1)}, bf16[128,512]{1,0:T(8,128)(2,1)}, bf16[128,512]{1,0:T(8,128)(2,1)}, bf16[128,512]{1,0:T(8,128)(2,1)}) custom-call(f32[2,128,128]{2,1,0:T(8,128)S(1)} %get-tuple-element.6.table_ref, bf16[4,128,128]{2,1,0:T(8,128)(2,1)S(1)} %collective-permute-done.1.refs_0_, ...), custom_call_target="tpu_custom_call" | custom-call | tf_op jit(solution)/shard_map/finish/pallas_call | solution.py:570
  (1 shorter events, 0.0 us)
Async XLA Ops:
  2.0 19.1 %copy-start.1 = (s32[6,2]{0,1:T(2,128)S(1)}, s32[6,2]{0,1:T(2,128)}, u32[]{:S(2)}) copy-start(s32[6,2]{0,1:T(2,128)} %param.14) | copy-start | bytes 148
  21.1 1.9 %copy-start = (s32[1024]{0:T(1024)S(1)}, s32[1024]{0:T(1024)}, u32[]{:S(2)}) copy-start(s32[1024]{0:T(1024)} %views_ref.1) | copy-start | bytes 12292
  21.1 1.9 %collective-permute-start = (bf16[16,128,128]{2,1,0:T(8,128)(2,1)S(1)}, bf16[16,128,128]{2,1,0:T(8,128)(2,1)S(1)}, u32[]{:S(2)}, u32[]{:S(2)}) collective-permute-start(bf16[16,128,128]{2,1,0:T(8,128)(2,1)S(1)} %all_to_all.5.mine_ref), channel_id=1, source_target_pairs={{0,1},{1,0},{2,3},{3,2},{4,5},{5,4},{6,7},{7,6},{8,9},{9,8},{10,11... | collective-permute-start | bytes 1572872 | tf_op jit(solution)/shard_map/ppermute | solution.py:534
  27.0 9.8 %collective-permute-start.4 = (bf16[4,128,128]{2,1,0:T(8,128)(2,1)S(1)}, bf16[4,128,128]{2,1,0:T(8,128)(2,1)S(1)}, u32[]{:S(2)}, u32[]{:S(2)}) collective-permute-start(bf16[4,128,128]{2,1,0:T(8,128)(2,1)S(1)} %get-tuple-element.8), channel_id=1, source_target_pairs={{0,16},{1,20},{2,18},{3,22},{4,17},{5,21},{6,19},{7,23},{8,24},{9,... | collective-permute-start | bytes 393224 | tf_op jit(solution)/shard_map/ppermute | solution.py:569
  30.3 11.2 %collective-permute-start.3 = (bf16[4,128,128]{2,1,0:T(8,128)(2,1)S(1)}, bf16[4,128,128]{2,1,0:T(8,128)(2,1)S(1)}, u32[]{:S(2)}, u32[]{:S(2)}) collective-permute-start(bf16[4,128,128]{2,1,0:T(8,128)(2,1)S(1)} %get-tuple-element.9), channel_id=1, source_target_pairs={{0,8},{1,12},{2,10},{3,14},{4,9},{5,13},{6,11},{7,15},{8,0},{9,4},... | collective-permute-start | bytes 393224 | tf_op jit(solution)/shard_map/ppermute | solution.py:569
  31.1 10.4 %collective-permute-start.2 = (bf16[4,128,128]{2,1,0:T(8,128)(2,1)S(1)}, bf16[4,128,128]{2,1,0:T(8,128)(2,1)S(1)}, u32[]{:S(2)}, u32[]{:S(2)}) collective-permute-start(bf16[4,128,128]{2,1,0:T(8,128)(2,1)S(1)} %get-tuple-element.10), channel_id=1, source_target_pairs={{0,0},{1,4},{2,2},{3,6},{4,1},{5,5},{6,3},{7,7},{8,8},{9,12},{10,1... | collective-permute-start | bytes 393224 | tf_op jit(solution)/shard_map/ppermute | solution.py:569
  31.7 9.8 %collective-permute-start.1 = (bf16[4,128,128]{2,1,0:T(8,128)(2,1)S(1)}, bf16[4,128,128]{2,1,0:T(8,128)(2,1)S(1)}, u32[]{:S(2)}, u32[]{:S(2)}) collective-permute-start(bf16[4,128,128]{2,1,0:T(8,128)(2,1)S(1)} %get-tuple-element.11), channel_id=1, source_target_pairs={{0,24},{1,28},{2,26},{3,30},{4,25},{5,29},{6,27},{7,31},{8,16},{9,... | collective-permute-start | bytes 393224 | tf_op jit(solution)/shard_map/ppermute | solution.py:569

commit v6 on v5

--- a/solution.py
+++ b/solution.py
@@ -232,7 +232,7 @@
 
 LOG2E = math.log2(math.e)
 VMEM_LIMIT = 48 * 1024 * 1024
-STANDING = {16: (11, 13, 10, 0, 2, 6, 7, 3, 4, 1, 15, 5, 9, 8, 12, 14)}
+STANDING = {16: (11, 13, 3, 2, 0, 6, 7, 5, 12, 1, 15, 10, 8, 9, 4, 14)}
 
 
 def whole(space=pltpu.VMEM):
@@ -342,6 +342,9 @@
     def turn(x):
         return lax.dot_general(eye, x, nt, preferred_element_type=jnp.float32).astype(jnp.bfloat16)
 
+    def flip(x):
+        return x.astype(jnp.float32).T.astype(jnp.bfloat16)
+
     for n, chip in enumerate(standing):
         stand_of[chip] = jnp.int32(n)
     for pos in range(blocks):
@@ -362,7 +365,7 @@
             there = slice(spot * block, (spot + 1) * block)
             kt_all[:, there] = turned[:, :block]
             vt_all[:HD, there] = turned[:, block:]
-        gt_all[:, here] = turn(g_all[here, :])
+        gt_all[:, here] = flip(g_all[here, :])
     vt_all[HD:, :] = jnp.ones((vt_all.shape[0] - HD, vt_all.shape[1]), jnp.bfloat16)
 
     second = lax.broadcasted_iota(jnp.int32, (1, wide), 1) >= block
@@ -384,8 +387,9 @@
             ok_a = ((far_a <= 1) | (far_a == count - 1)).astype(jnp.int32)
             ok_b = ((far_b <= 1) | (far_b == count - 1)).astype(jnp.int32)
             oks[tile].append(jnp.where(second, ok_b, ok_a) > 0)
-    owned = [place_of[2 * jnp.bitwise_xor(slab, m) + core] for m in range(out_ref.shape[0])]
-    levels, deltas, sums = {}, {}, [0, 0]
+    slabs = out_ref.shape[0]
+    owned = [place_of[2 * jnp.bitwise_xor(slab, m) + core] for m in range(slabs)]
+    levels, shares, deltas, sums = {}, {}, {}, [0, 0]
 
     def scores(tile):
         top = jnp.full((1, wide), NEG, jnp.float32)
@@ -405,10 +409,10 @@
     def outputs(tile):
         out = jnp.dot(vt_all[:, windows[tile]], e_all[tile], preferred_element_type=jnp.float32)
         total = out[HD : HD + 1, :]
-        out = out[:HD, :] / total
+        shares[tile] = 1.0 / total
+        out = out[:HD, :] * shares[tile]
         at_all[:, lanes[tile]] = out.astype(jnp.bfloat16)
         deltas[tile] = jnp.sum(gt_all[:, lanes[tile]].astype(jnp.float32) * out, axis=0, keepdims=True)
-        levels[tile] = levels[tile] + jnp.log2(total)
 
     def slopes(tile):
         for i in range(span):
@@ -416,7 +420,7 @@
             d = lax.dot_general(
                 kv_all[pl.ds(places[tile][i] + block, block), :], g_all[lanes[tile], :], nt, preferred_element_type=jnp.float32
             )
-            p = jnp.exp2(s_all[tile, i] * factor - jnp.where(oks[tile][i], levels[tile], -NEG))
+            p = e_all[tile, here, :].astype(jnp.float32) * shares[tile]
             p_all[tile, here, :] = p.astype(jnp.bfloat16)
             ds_all[tile, here, :] = (p * (d - deltas[tile])).astype(jnp.bfloat16)
         p_all[tile, span * block :, :] = jnp.zeros((block, wide), jnp.bfloat16)
@@ -462,8 +466,8 @@
     dk, dv = sums
     for m, pos in enumerate(owned):
         here = pl.ds(pl.multiple_of(pos * block, block), block)
-        out_ref[m, 0] = turn(at_all[:, here])
-        out_ref[m, 1] = turn(dq_all[:, here])
+        out_ref[m, 0] = flip(at_all[:, here])
+        out_ref[m, 1] = flip(dq_all[:, here])
         out_ref[m, 2] = (dk[m * block : (m + 1) * block] * scale).astype(jnp.bfloat16)
         out_ref[m, 3] = dv[m * block : (m + 1) * block].astype(jnp.bfloat16)
 
@@ -473,7 +477,8 @@
     slab = slab_of()
     cosine, sine = table_ref[0], table_ref[1]
     for m, ref in zip(turns, chunks, strict=True):
-        lanes = pl.ds(pl.multiple_of(jnp.bitwise_xor(slab, m) * HD, HD), HD)
+        head = jnp.bitwise_xor(slab, m)
+        lanes = pl.ds(pl.multiple_of(head * HD, HD), HD)
         for at, out in enumerate(outs):
             x = ref[at]
             if at in (1, 2):
@@ -597,7 +602,6 @@
             seqs * parts == 2 * heads
             and seqs % 2 == 0
             and parts % 2 == 0
-            and seqs & (seqs - 1) == 0
             and count <= seqs < 2 * count
             and count_span(count, seqs) <= seqs
         )

time: 43.1 us -> 42.1 us (0.977)
  the two profiles are of different devices: /device:TPU:0 before, /device:TPU:1 now
where the time goes in v6:
time: 42.1 us; the launch traced here: 41.9 us
  blocking collectives  18.6 us (44%)
  starting transfers between devices  10.2 us (24%)
  waiting for transfers between devices  6.31 us (15%)
  Pallas kernels  5.99 us (14%)
  between operations  0.67 us (2%)
    all_to_all x1, blocking collectives, by_chip(): lax.all_to_all(sent, axes, 0, 0, axis_index_groups=same_core, tiled=True)  18.6 us
    ppermute x4, starting transfers between devices, by_chip(): chunks = [lax.ppermute(back[m], axes, route(m)) for m in turns]  8.21 us
    ppermute x4, waiting for transfers between devices, by_chip(): chunks = [lax.ppermute(back[m], axes, route(m)) for m in turns]  4.87 us
    pallas_call x1, Pallas kernels, by_chip(): pl.pallas_call(functools.partial(attend_kernel, core_of, slab_of, standin...  3.71 us
    ppermute x1, starting transfers between devices, by_chip(): other = lax.ppermute(mine, axes, [(d, d ^ 1) for d in range(seqs * parts)])  2 us
    ppermute x1, waiting for transfers between devices, by_chip(): other = lax.ppermute(mine, axes, [(d, d ^ 1) for d in range(seqs * parts)])  1.44 us
    pallas_call x1, Pallas kernels, by_chip(): pl.pallas_call(functools.partial(prepare_kernel, row_first, head_of), out...  1.37 us
    pallas_call x1, Pallas kernels, by_chip(): pl.pallas_call(functools.partial(finish_kernel, slab_of, turns), out_shap...  0.91 us
  transfers between devices with their start and end apart: 5, of which 4 were waited for; matrix products, arithmetic and copies ran while one was open for 0% of the time, Pallas kernels for 0%

profile of v6, /device:TPU:1, one launch (start us, length us, event | category | flops | bytes accessed | tf_op | source)
XLA Modules:
  0.0 41.9 jit_solution(16457049560811806548)
XLA Ops:
  0.6 1.4 %prepare.1 = (bf16[16,128,128]{2,1,0:T(8,128)(2,1)S(1)}, f32[2,128,128]{2,1,0:T(8,128)S(1)}) custom-call(s32[3,128]{1,0:T(4,128)} %pos_hbm.1, f32[64,8]{1,0:T(8,128)} %constant.2.clone.step_hbm, bf16[32,2048]{1,0:T(8,128)(2,1)} %q_hbm.1, bf16[32,2048]{1,0:T(8,128)(2,1)} %k_hbm.1, bf16[32,2048]{1,0:T(8,128)(2,1)} %v_hbm.1, bf16[32,2048]{1,0:T(8,128)(2,1)} %g_hbm.1), custom_call_target="tpu_custom_call" | custom-call | tf_op jit(solution)/shard_map/prepare/pallas_call | solution.py:519
  2.0 0.0 copy-start.1
  2.0 18.6 %all_to_all.5.mine_ref = bf16[16,128,128]{2,1,0:T(8,128)(2,1)S(1)} all-to-all(bf16[16,128,128]{2,1,0:T(8,128)(2,1)S(1)} %get-tuple-element.7), channel_id=1, replica_groups={{22,26,6,4,0,12,14,10,24,2,30,20,16,18,8,28},{23,27,7,5,1,13,15,11,25,3..., dimensions={0} | all-to-all | bytes 1048576 | tf_op jit(solution)/shard_map/all_to_all | solution.py:538
  20.6 0.0 copy-start
  20.6 2.0 %collective-permute-start = (bf16[16,128,128]{2,1,0:T(8,128)(2,1)S(1)}, bf16[16,128,128]{2,1,0:T(8,128)(2,1)S(1)}, u32[]{:S(2)}, u32[]{:S(2)}) collective-permute-start(bf16[16,128,128]{2,1,0:T(8,128)(2,1)S(1)} %all_to_all.5.mine_ref), channel_id=1, source_target_pairs={{0,1},{1,0},{2,3},{3,2},{4,5},{5,4},{6,7},{7,6},{8,9},{9,8},{10,11... | collective-permute-start | bytes 1572872 | tf_op jit(solution)/shard_map/ppermute | solution.py:539
  22.6 0.0 copy-done.1
  22.6 0.1 copy.12.near_ref
  22.7 1.4 %collective-permute-done.other_ref = bf16[16,128,128]{2,1,0:T(8,128)(2,1)S(1)} collective-permute-done((bf16[16,128,128]{2,1,0:T(8,128)(2,1)S(1)}, bf16[16,128,128]{2,1,0:T(8,128)(2,1)S(1)}, u32[]{:S(2)}, u32[]{:S(2)}) %collective-permute-start) | collective-permute-done | bytes 524320 | tf_op jit(solution)/shard_map/ppermute | solution.py:539
  24.1 0.0 copy-done
  24.1 3.7 %attend.1 = bf16[4,4,128,128]{3,2,1,0:T(8,128)(2,1)S(1)} custom-call(s32[1024]{0:T(1024)S(1)} %copy-done, s32[6,2]{1,0:T(8,128)S(1)} %copy.12.near_ref, bf16[16,128,128]{2,1,0:T(8,128)(2,1)S(1)} %all_to_all.5.mine_ref, bf16[16,128,128]{2,1,0:T(8,128)(2,1)S(1)} %collective-permute-done.other_ref), custom_call_target="tpu_custom_call" | custom-call | tf_op jit(solution)/shard_map/attend/pallas_call | solution.py:540
  27.9 2.1 %collective-permute-start.4 = (bf16[4,128,128]{2,1,0:T(8,128)(2,1)S(1)}, bf16[4,128,128]{2,1,0:T(8,128)(2,1)S(1)}, u32[]{:S(2)}, u32[]{:S(2)}) collective-permute-start(bf16[4,128,128]{2,1,0:T(8,128)(2,1)S(1)} %get-tuple-element.8), channel_id=1, source_target_pairs={{0,16},{1,20},{2,18},{3,22},{4,17},{5,21},{6,19},{7,23},{8,24},{9,... | collective-permute-start | bytes 393224 | tf_op jit(solution)/shard_map/ppermute | solution.py:574
  29.9 1.9 %collective-permute-start.3 = (bf16[4,128,128]{2,1,0:T(8,128)(2,1)S(1)}, bf16[4,128,128]{2,1,0:T(8,128)(2,1)S(1)}, u32[]{:S(2)}, u32[]{:S(2)}) collective-permute-start(bf16[4,128,128]{2,1,0:T(8,128)(2,1)S(1)} %get-tuple-element.9), channel_id=1, source_target_pairs={{0,8},{1,12},{2,10},{3,14},{4,9},{5,13},{6,11},{7,15},{8,0},{9,4},... | collective-permute-start | bytes 393224 | tf_op jit(solution)/shard_map/ppermute | solution.py:574
  31.8 1.9 %collective-permute-start.2 = (bf16[4,128,128]{2,1,0:T(8,128)(2,1)S(1)}, bf16[4,128,128]{2,1,0:T(8,128)(2,1)S(1)}, u32[]{:S(2)}, u32[]{:S(2)}) collective-permute-start(bf16[4,128,128]{2,1,0:T(8,128)(2,1)S(1)} %get-tuple-element.10), channel_id=1, source_target_pairs={{0,0},{1,4},{2,2},{3,6},{4,1},{5,5},{6,3},{7,7},{8,8},{9,12},{10,1... | collective-permute-start | bytes 393224 | tf_op jit(solution)/shard_map/ppermute | solution.py:574
  33.7 2.4 %collective-permute-start.1 = (bf16[4,128,128]{2,1,0:T(8,128)(2,1)S(1)}, bf16[4,128,128]{2,1,0:T(8,128)(2,1)S(1)}, u32[]{:S(2)}, u32[]{:S(2)}) collective-permute-start(bf16[4,128,128]{2,1,0:T(8,128)(2,1)S(1)} %get-tuple-element.11), channel_id=1, source_target_pairs={{0,24},{1,28},{2,26},{3,30},{4,25},{5,29},{6,27},{7,31},{8,16},{9,... | collective-permute-start | bytes 393224 | tf_op jit(solution)/shard_map/ppermute | solution.py:574
  36.1 2.8 %collective-permute-done.4.refs_3_ = bf16[4,128,128]{2,1,0:T(8,128)(2,1)S(1)} collective-permute-done((bf16[4,128,128]{2,1,0:T(8,128)(2,1)S(1)}, bf16[4,128,128]{2,1,0:T(8,128)(2,1)S(1)}, u32[]{:S(2)}, u32[]{:S(2)}) %collective-permute-start.4) | collective-permute-done | bytes 131104 | tf_op jit(solution)/shard_map/ppermute | solution.py:574
  38.9 0.0 collective-permute-done.3.refs_2_
  38.9 0.4 collective-permute-done.2.refs_1_
  39.3 1.7 %collective-permute-done.1.refs_0_ = bf16[4,128,128]{2,1,0:T(8,128)(2,1)S(1)} collective-permute-done((bf16[4,128,128]{2,1,0:T(8,128)(2,1)S(1)}, bf16[4,128,128]{2,1,0:T(8,128)(2,1)S(1)}, u32[]{:S(2)}, u32[]{:S(2)}) %collective-permute-start.1) | collective-permute-done | bytes 131104 | tf_op jit(solution)/shard_map/ppermute | solution.py:574
  41.0 0.9 %finish.1 = (bf16[128,512]{1,0:T(8,128)(2,1)}, bf16[128,512]{1,0:T(8,128)(2,1)}, bf16[128,512]{1,0:T(8,128)(2,1)}, bf16[128,512]{1,0:T(8,128)(2,1)}) custom-call(f32[2,128,128]{2,1,0:T(8,128)S(1)} %get-tuple-element.6.table_ref, bf16[4,128,128]{2,1,0:T(8,128)(2,1)S(1)} %collective-permute-done.1.refs_0_, ...), custom_call_target="tpu_custom_call" | custom-call | tf_op jit(solution)/shard_map/finish/pallas_call | solution.py:575
  (1 shorter events, 0.0 us)
Async XLA Ops:
  2.0 20.6 %copy-start.1 = (s32[6,2]{0,1:T(2,128)S(1)}, s32[6,2]{0,1:T(2,128)}, u32[]{:S(2)}) copy-start(s32[6,2]{0,1:T(2,128)} %param.14) | copy-start | bytes 148
  20.6 3.5 %copy-start = (s32[1024]{0:T(1024)S(1)}, s32[1024]{0:T(1024)}, u32[]{:S(2)}) copy-start(s32[1024]{0:T(1024)} %views_ref.1) | copy-start | bytes 12292
  20.6 3.5 %collective-permute-start = (bf16[16,128,128]{2,1,0:T(8,128)(2,1)S(1)}, bf16[16,128,128]{2,1,0:T(8,128)(2,1)S(1)}, u32[]{:S(2)}, u32[]{:S(2)}) collective-permute-start(bf16[16,128,128]{2,1,0:T(8,128)(2,1)S(1)} %all_to_all.5.mine_ref), channel_id=1, source_target_pairs={{0,1},{1,0},{2,3},{3,2},{4,5},{5,4},{6,7},{7,6},{8,9},{9,8},{10,11... | collective-permute-start | bytes 1572872 | tf_op jit(solution)/shard_map/ppermute | solution.py:539
  27.9 11.1 %collective-permute-start.4 = (bf16[4,128,128]{2,1,0:T(8,128)(2,1)S(1)}, bf16[4,128,128]{2,1,0:T(8,128)(2,1)S(1)}, u32[]{:S(2)}, u32[]{:S(2)}) collective-permute-start(bf16[4,128,128]{2,1,0:T(8,128)(2,1)S(1)} %get-tuple-element.8), channel_id=1, source_target_pairs={{0,16},{1,20},{2,18},{3,22},{4,17},{5,21},{6,19},{7,23},{8,24},{9,... | collective-permute-start | bytes 393224 | tf_op jit(solution)/shard_map/ppermute | solution.py:574
  29.9 9.0 %collective-permute-start.3 = (bf16[4,128,128]{2,1,0:T(8,128)(2,1)S(1)}, bf16[4,128,128]{2,1,0:T(8,128)(2,1)S(1)}, u32[]{:S(2)}, u32[]{:S(2)}) collective-permute-start(bf16[4,128,128]{2,1,0:T(8,128)(2,1)S(1)} %get-tuple-element.9), channel_id=1, source_target_pairs={{0,8},{1,12},{2,10},{3,14},{4,9},{5,13},{6,11},{7,15},{8,0},{9,4},... | collective-permute-start | bytes 393224 | tf_op jit(solution)/shard_map/ppermute | solution.py:574
  31.8 7.5 %collective-permute-start.2 = (bf16[4,128,128]{2,1,0:T(8,128)(2,1)S(1)}, bf16[4,128,128]{2,1,0:T(8,128)(2,1)S(1)}, u32[]{:S(2)}, u32[]{:S(2)}) collective-permute-start(bf16[4,128,128]{2,1,0:T(8,128)(2,1)S(1)} %get-tuple-element.10), channel_id=1, source_target_pairs={{0,0},{1,4},{2,2},{3,6},{4,1},{5,5},{6,3},{7,7},{8,8},{9,12},{10,1... | collective-permute-start | bytes 393224 | tf_op jit(solution)/shard_map/ppermute | solution.py:574
  33.7 7.3 %collective-permute-start.1 = (bf16[4,128,128]{2,1,0:T(8,128)(2,1)S(1)}, bf16[4,128,128]{2,1,0:T(8,128)(2,1)S(1)}, u32[]{:S(2)}, u32[]{:S(2)}) collective-permute-start(bf16[4,128,128]{2,1,0:T(8,128)(2,1)S(1)} %get-tuple-element.11), channel_id=1, source_target_pairs={{0,24},{1,28},{2,26},{3,30},{4,25},{5,29},{6,27},{7,31},{8,16},{9,... | collective-permute-start | bytes 393224 | tf_op jit(solution)/shard_map/ppermute | solution.py:574
